TPU v7x, 512 devices: a whole 4x4x16 slice. The times are simulated.
512 devices in a mesh: image: 16 (over x, y), space: 32 (over z, core).
Axes of the slice: x: 4, y: 4, z: 16, core: 2. Of those that a mesh axis runs over, the one named last changes fastest.
Arguments:
- positions: float32 [16, 3, 32768], P('image', None, 'space'), may hold values from -20 to 20
- neighbours: int32 [256, 3], replicated, may hold values from 0 to 4
- brackets: int32 [16], P('image'), may hold values from 0 to 14, as said below
- codes: int32 [16], P('image'), may hold values from 0 to 65535
Outputs:
- new_images: float32 [16, 3, 32768], P('image', None, 'space')
- arc_fraction: float32 [16], P('image')
Inputs may be any that keep to these rules, and one draw needn't show every extreme that they name: brackets[j] lies between j - 1 and j + 1 - 1; both ends of that window are reached.
All inputs are finite; a program needn't handle non-finite values.
Results may differ from a plain program's by a relative error of at most 0.0003.
Values sent between devices are 32-bit elements; how exact they have to be, the bound alone decides.
A program may use at most 64 MiB of HBM per device.

v0:
```python
import jax
import jax.numpy as jnp
from jax import lax
from jax.sharding import PartitionSpec as P

PROT_DEV = 128
BLOCK = 128
HALO = 2
STEPS = 10


TIME_STEP = 0.05
RESTRAINT = 1.0
COUPLING = 3.0
KERNEL_RATE = 0.125
EPSILON = 1e-06
CODE_SCALE = 65536.0


def extended(cells, sides, width, closed):
    for axis, dim in sides:
        count = lax.axis_size(axis)
        ends = count if closed else count - 1
        head = lax.slice_in_dim(cells, 0, width, axis=dim)
        tail = lax.slice_in_dim(cells, cells.shape[dim] - width, cells.shape[dim], axis=dim)
        cells = jnp.concatenate(
            [
                lax.ppermute(tail, axis, [(i, (i + 1) % count) for i in range(ends)]),
                cells,
                lax.ppermute(head, axis, [((i + 1) % count, i) for i in range(ends)]),
            ],
            axis=dim,
        )
    return cells


def passed_along(block, axis, distance):
    devices = range(lax.axis_size(axis))
    route = [(i - distance, i) for i in devices if i - distance in devices]
    return lax.ppermute(block, axis, route)


def from_everyone(value, axis):
    copies = jnp.broadcast_to(value, (lax.axis_size(axis), *value.shape))
    return lax.all_to_all(copies, axis, split_axis=0, concat_axis=0, tiled=True)


def taken_together(value, axis):
    return from_everyone(value, axis).sum(axis=0)


def in_order(pieces, dim):
    lengths = list(pieces.shape[1:])
    lengths[dim] *= pieces.shape[0]
    return jnp.moveaxis(pieces, 0, dim).reshape(lengths)


def gather_directly(value, axis, dim):
    pieces = from_everyone(value, axis)
    return in_order(pieces, dim)


def pair_forces(swarm_centres, partner_beads):
    centre_sq = jnp.sum(swarm_centres * swarm_centres, axis=-3)
    partner_sq = jnp.sum(partner_beads * partner_beads, axis=-3)
    crossing_flags = jnp.einsum(
        "...euh,...euw->...uhw", swarm_centres, partner_beads, precision=lax.Precision.HIGHEST
    )
    weight_factors = jnp.exp(
        -KERNEL_RATE * (centre_sq[..., :, None] + partner_sq[..., None, :] - 2.0 * crossing_flags)
    )
    row_sums = jnp.sum(weight_factors, axis=-1)
    pulled_images = jnp.einsum(
        "...aun,...san->...sau", weight_factors, partner_beads, precision=lax.Precision.HIGHEST
    )
    return (
        COUPLING
        / partner_beads.shape[-1]
        * (swarm_centres * row_sums[..., None, :, :] - pulled_images)
    )


def block_forces(widened, offset_table, centre_count):
    block_beads = widened.shape[3]
    partner_count = offset_table.shape[1]
    partner_rows = jnp.arange(centre_count, dtype=jnp.int32)[:, None] + offset_table
    centres = widened[..., HALO : HALO + centre_count, :]
    partners = jnp.take(widened, partner_rows, axis=-2)
    lead = partners.shape[:-3]
    partners = partners.reshape(lead + (centre_count, partner_count * block_beads))
    return pair_forces(centres, partners)


def body(positions, neighbours, brackets, codes):
    per_device = positions.shape[0]
    slab_beads = positions.shape[2]
    blocks_own = slab_beads // BLOCK
    slab_id = lax.axis_index("space")
    total_blocks = lax.axis_size("space") * blocks_own
    bead_index = jnp.arange(slab_beads, dtype=jnp.int32).reshape(blocks_own, BLOCK)
    restrain = (bead_index < PROT_DEV).astype(jnp.float32)
    anchor = positions.reshape(per_device, 3, blocks_own, BLOCK)
    own_table = lax.dynamic_slice_in_dim(neighbours, slab_id * blocks_own, blocks_own, 0)
    widened_count = blocks_own + 4 * HALO
    middle = blocks_own + 2 * HALO

    def deep_rims(state_now):
        padded = extended(state_now, (("space", 2),), 2 * HALO * BLOCK, True)
        return padded.reshape(per_device, 3, widened_count, BLOCK)

    row_ids = (slab_id * blocks_own - HALO + jnp.arange(middle, dtype=jnp.int32)) % total_blocks
    middle_table = jnp.take(neighbours, row_ids, axis=0)
    wide_blocks = (jnp.arange(widened_count, dtype=jnp.int32) - 2 * HALO) % blocks_own
    wide_beads = wide_blocks[:, None] * BLOCK + jnp.arange(BLOCK, dtype=jnp.int32)[None, :]
    middle_restrain = (wide_beads[HALO : HALO + middle] < PROT_DEV).astype(jnp.float32)
    middle_anchor = deep_rims(positions)[:, :, HALO : HALO + middle]

    def advance_pair(turn_index, current):
        widened = deep_rims(current)
        centre = widened[:, :, HALO : HALO + middle]
        forces = block_forces(widened, middle_table, middle)
        stepped = centre + TIME_STEP * (
            forces - RESTRAINT * middle_restrain * (centre - middle_anchor)
        )
        owned = stepped[:, :, HALO : HALO + blocks_own]
        forces = block_forces(stepped, own_table, blocks_own)
        advanced = owned + TIME_STEP * (forces - RESTRAINT * restrain * (owned - anchor))
        return advanced.reshape(per_device, 3, slab_beads)

    evolved = lax.fori_loop(0, STEPS // 2, advance_pair, positions)
    protein = evolved[:, :, :PROT_DEV]
    before = passed_along(protein[per_device - 1], "image", 1)
    earlier = jnp.concatenate([before[None], protein[: per_device - 1]], axis=0)
    differences = protein - earlier
    partial_value = jnp.sum(differences * differences, axis=(1, 2))
    squares = taken_together(partial_value, "space")
    image_count = lax.axis_size("image") * per_device
    first_id = lax.axis_index("image") * per_device
    global_ids = first_id + jnp.arange(per_device, dtype=jnp.int32)
    step_length = jnp.where(global_ids > 0, jnp.sqrt(squares + EPSILON), 0.0)
    all_steps = gather_directly(step_length, "image", 0)
    arc_all = jnp.cumsum(all_steps)
    length_total = arc_all[image_count - 1]
    arc_here = lax.dynamic_slice_in_dim(arc_all, first_id, per_device)
    old_images = extended(evolved, (("image", 0),), per_device, False)
    arc_values = extended(arc_here, (("image", 0),), per_device, False)
    root = first_id - per_device
    local_index = brackets - root
    places = jnp.arange(old_images.shape[0], dtype=jnp.int32)
    lower_pick = (places[None, :] == local_index[:, None]).astype(jnp.float32)
    upper_pick = (places[None, :] == local_index[:, None] + 1).astype(jnp.float32)
    arc_lower = jnp.sum(lower_pick * arc_values[None, :], axis=1)
    upper_arc_bound = jnp.sum(upper_pick * arc_values[None, :], axis=1)
    target = (brackets.astype(jnp.float32) + codes.astype(jnp.float32) / CODE_SCALE) / (
        image_count - 1
    )
    weight = (target * length_total - arc_lower) / (upper_arc_bound - arc_lower)
    mixing = (1.0 - weight)[:, None] * lower_pick + weight[:, None] * upper_pick
    new_images = jnp.einsum("ie,ecb->icb", mixing, old_images, precision=lax.Precision.HIGHEST)
    return (new_images, arc_here / length_total)


def solution(mesh):
    placed = (P("image", None, "space"), P(), P("image"), P("image"))
    return jax.shard_map(
        body,
        mesh=mesh,
        in_specs=placed,
        out_specs=(P("image", None, "space"), P("image")),
        check_vma=False,
    )
```

profile of v0, /device:TPU:24, one launch (start us, length us, event | category | flops | bytes accessed | tf_op | source)
XLA Modules:
  0.0 157.1 jit_solution(16568816343721891646)
XLA Ops:
  0.6 0.7 fusion.57
  1.3 8.9 %collective-permute-start.3 = (f32[1,3,512]{2,0,1:T(1,128)S(1)}, f32[1,3,512]{2,0,1:T(1,128)S(1)}, u32[]{:S(2)}, u32[]{:S(2)}) collective-permute-start(f32[1,3,512]{2,0,1:T(1,128)S(1)} %get-tuple-element.126), channel_id=1, source_target_pairs={{1,0},{2,1},{3,2},{4,3},{5,4},{6,5},{7,6},{8,7},{9,8},{10,9},{11,1... | collective-permute-start | bytes 18440 | tf_op jit(solution)/shard_map/ppermute | solution.py:30
  10.3 0.8 copy.70
  11.3 0.6 gather_fusion.2
  12.0 0.8 constant_dynamic-slice_fusion.1
  12.7 0.7 copy.71
  13.5 0.7 copy.74
  14.2 0.7 pad_maximum_fusion.1
  15.0 79.4 %while.11 = (s32[]{:T(128)}, f32[1,3,1024]{2,1,0:T(4,128)S(1)}, s32[12,3]{0,1:T(4,128)S(1)}, f32[12,128]{1,0:T(8,128)S(1)}, f32[1,3,12,128]{3,1,2,0:T(4,128)S(1)...) while((s32[]{:T(128)}, f32[1,3,1024]{2,1,0:T(4,128)S(1)}, ...), condition=%wide.region_7.8_spmd.clone, body=%wide.region_0.7_spmd.clone.sunk | while | flops 75880080 | bytes 8957014 | solution.py:130
  15.1 2.9 %collective-permute-start.1 = (f32[1,3,512]{2,1,0:T(4,128)S(1)}, f32[1,3,512]{2,1,0:T(4,128)S(1)}, u32[]{:S(2)}, u32[]{:S(2)}) collective-permute-start(f32[1,3,512]{2,1,0:T(4,128)S(1)} %get-tuple-element.179), channel_id=1, source_target_pairs={{1,0},{2,1},{3,2},{4,3},{5,4},{6,5},{7,6},{8,7},{9,8},{10,9},{11,1... | collective-permute-start | bytes 18440 | tf_op jit(solution)/shard_map/while/body/eval_jaxpr/ppermute | solution.py:30
  19.4 0.6 gather_fusion
  20.2 3.3 %fusion.74 = (f32[12,128]{1,0:T(8,128)S(1)}, f32[12,128,384]{2,1,0:T(8,128)S(1)}) fusion(f32[3,12,384]{2,0,1:T(4,128)S(1)} %bitcast.154, pred[12,384]{1,0:T(8,128)(4,1)S(1)} %bitcast.168, f32[1,3,16,128]{3,1,2,0:T(4,128)S(1)} %bitcast.158, f32[12,384]{1,0:T(8,128)S(1)} %bitcast.167, f32[12,128]{1,0:T(8,128)S(1)} %multiply_reduce_fusion.9), kind=kOutput, calls=%fused_computation.106.clone.1 | convolution fusion | flops 24195072 | bytes 2502656 | tf_op jit(solution)/shard_map/while/body/eval_jaxpr/...euh,...euw->...uhw/dot_general | solution.py:66
  23.5 2.6 %multiply_add_fusion.2 = f32[1,3,12,128]{3,1,2,0:T(4,128)S(1)} fusion(f32[1,3,12,128]{3,1,2,0:T(4,128)S(1)} %get-tuple-element.208, f32[1,3,16,128]{3,1,2,0:T(4,128)S(1)} %bitcast.159, f32[12,128]{1,0:T(8,128)S(1)} %get-tuple-element.207, f32[12,128]{1,0:T(8,128)S(1)} %get-tuple-element.180, f32[12,128,384]{2,1,0:T(8,128)S(1)} %get-tuple-element.181, ...), kind=kOutput, calls=%fused_computation.27.clone.1 | convolution fusion | flops 21284352 | bytes 2486784 | tf_op jit(solution)/shard_map/while/body/eval_jaxpr/...aun,...san->...sau/dot_general | solution.py:73
  26.1 0.6 gather_fusion.1
  26.8 2.3 %fusion.75 = (f32[8,128]{1,0:T(8,128)S(1)}, f32[8,128,384]{2,1,0:T(8,128)S(1)}) fusion(f32[3,8,384]{2,0,1:T(4,128)S(1)} %bitcast.162, pred[8,384]{1,0:T(8,128)(4,1)S(1)} %broadcast_bitcast_fusion.2, f32[1,3,12,128]{3,1,2,0:T(4,128)S(1)} %multiply_add_fusion.2, f32[8,384]{1,0:T(8,128)S(1)} %bitcast.170, f32[8,128]{1,0:T(8,128)S(1)} %multiply_reduce_fusion.11), kind=kOutput, calls=%fused_computation.107.clone.1 | convolution fusion | flops 16130048 | bytes 1661952 | tf_op jit(solution)/shard_map/while/body/eval_jaxpr/...euh,...euw->...uhw/dot_general | solution.py:66
  29.1 1.8 %fusion.77 = f32[1,3,1024]{2,1,0:T(4,128)S(1)} fusion(f32[8,128,384]{2,1,0:T(8,128)S(1)} %get-tuple-element.182, f32[3,8,384]{2,0,1:T(4,128)S(1)} %bitcast.163, pred[8,384]{1,0:T(8,128)(4,1)S(1)} %broadcast_bitcast_fusion.2, f32[1,3,8,128]{3,1,2,0:T(4,128)S(1)} %get-tuple-element.210, f32[1,3,12,128]{3,1,2,0:T(4,128)S(1)} %multiply_add_fusion.2, ...), kind=kOutput, calls=%fused_computation.13.clone.1 | convolution fusion | flops 14189568 | bytes 1657856 | tf_op jit(solution)/shard_map/while/body/eval_jaxpr/...aun,...san->...sau/dot_general | solution.py:73
  30.9 2.9 %collective-permute-start.1 = (f32[1,3,512]{2,1,0:T(4,128)S(1)}, f32[1,3,512]{2,1,0:T(4,128)S(1)}, u32[]{:S(2)}, u32[]{:S(2)}) collective-permute-start(f32[1,3,512]{2,1,0:T(4,128)S(1)} %get-tuple-element.179), channel_id=1, source_target_pairs={{1,0},{2,1},{3,2},{4,3},{5,4},{6,5},{7,6},{8,7},{9,8},{10,9},{11,1... | collective-permute-start | bytes 18440 | tf_op jit(solution)/shard_map/while/body/eval_jaxpr/ppermute | solution.py:30
  34.7 0.5 collective-permute-done
  35.3 0.6 gather_fusion
  36.1 3.3 %fusion.74 = (f32[12,128]{1,0:T(8,128)S(1)}, f32[12,128,384]{2,1,0:T(8,128)S(1)}) fusion(f32[3,12,384]{2,0,1:T(4,128)S(1)} %bitcast.154, pred[12,384]{1,0:T(8,128)(4,1)S(1)} %bitcast.168, f32[1,3,16,128]{3,1,2,0:T(4,128)S(1)} %bitcast.158, f32[12,384]{1,0:T(8,128)S(1)} %bitcast.167, f32[12,128]{1,0:T(8,128)S(1)} %multiply_reduce_fusion.9), kind=kOutput, calls=%fused_computation.106.clone.1 | convolution fusion | flops 24195072 | bytes 2502656 | tf_op jit(solution)/shard_map/while/body/eval_jaxpr/...euh,...euw->...uhw/dot_general | solution.py:66
  39.4 2.6 %multiply_add_fusion.2 = f32[1,3,12,128]{3,1,2,0:T(4,128)S(1)} fusion(f32[1,3,12,128]{3,1,2,0:T(4,128)S(1)} %get-tuple-element.208, f32[1,3,16,128]{3,1,2,0:T(4,128)S(1)} %bitcast.159, f32[12,128]{1,0:T(8,128)S(1)} %get-tuple-element.207, f32[12,128]{1,0:T(8,128)S(1)} %get-tuple-element.180, f32[12,128,384]{2,1,0:T(8,128)S(1)} %get-tuple-element.181, ...), kind=kOutput, calls=%fused_computation.27.clone.1 | convolution fusion | flops 21284352 | bytes 2486784 | tf_op jit(solution)/shard_map/while/body/eval_jaxpr/...aun,...san->...sau/dot_general | solution.py:73
  42.0 0.6 gather_fusion.1
  42.7 2.3 %fusion.75 = (f32[8,128]{1,0:T(8,128)S(1)}, f32[8,128,384]{2,1,0:T(8,128)S(1)}) fusion(f32[3,8,384]{2,0,1:T(4,128)S(1)} %bitcast.162, pred[8,384]{1,0:T(8,128)(4,1)S(1)} %broadcast_bitcast_fusion.2, f32[1,3,12,128]{3,1,2,0:T(4,128)S(1)} %multiply_add_fusion.2, f32[8,384]{1,0:T(8,128)S(1)} %bitcast.170, f32[8,128]{1,0:T(8,128)S(1)} %multiply_reduce_fusion.11), kind=kOutput, calls=%fused_computation.107.clone.1 | convolution fusion | flops 16130048 | bytes 1661952 | tf_op jit(solution)/shard_map/while/body/eval_jaxpr/...euh,...euw->...uhw/dot_general | solution.py:66
  45.0 1.8 %fusion.77 = f32[1,3,1024]{2,1,0:T(4,128)S(1)} fusion(f32[8,128,384]{2,1,0:T(8,128)S(1)} %get-tuple-element.182, f32[3,8,384]{2,0,1:T(4,128)S(1)} %bitcast.163, pred[8,384]{1,0:T(8,128)(4,1)S(1)} %broadcast_bitcast_fusion.2, f32[1,3,8,128]{3,1,2,0:T(4,128)S(1)} %get-tuple-element.210, f32[1,3,12,128]{3,1,2,0:T(4,128)S(1)} %multiply_add_fusion.2, ...), kind=kOutput, calls=%fused_computation.13.clone.1 | convolution fusion | flops 14189568 | bytes 1657856 | tf_op jit(solution)/shard_map/while/body/eval_jaxpr/...aun,...san->...sau/dot_general | solution.py:73
  46.8 2.9 %collective-permute-start.1 = (f32[1,3,512]{2,1,0:T(4,128)S(1)}, f32[1,3,512]{2,1,0:T(4,128)S(1)}, u32[]{:S(2)}, u32[]{:S(2)}) collective-permute-start(f32[1,3,512]{2,1,0:T(4,128)S(1)} %get-tuple-element.179), channel_id=1, source_target_pairs={{1,0},{2,1},{3,2},{4,3},{5,4},{6,5},{7,6},{8,7},{9,8},{10,9},{11,1... | collective-permute-start | bytes 18440 | tf_op jit(solution)/shard_map/while/body/eval_jaxpr/ppermute | solution.py:30
  50.6 0.5 collective-permute-done
  51.1 0.6 gather_fusion
  52.0 3.3 %fusion.74 = (f32[12,128]{1,0:T(8,128)S(1)}, f32[12,128,384]{2,1,0:T(8,128)S(1)}) fusion(f32[3,12,384]{2,0,1:T(4,128)S(1)} %bitcast.154, pred[12,384]{1,0:T(8,128)(4,1)S(1)} %bitcast.168, f32[1,3,16,128]{3,1,2,0:T(4,128)S(1)} %bitcast.158, f32[12,384]{1,0:T(8,128)S(1)} %bitcast.167, f32[12,128]{1,0:T(8,128)S(1)} %multiply_reduce_fusion.9), kind=kOutput, calls=%fused_computation.106.clone.1 | convolution fusion | flops 24195072 | bytes 2502656 | tf_op jit(solution)/shard_map/while/body/eval_jaxpr/...euh,...euw->...uhw/dot_general | solution.py:66
  55.2 2.6 %multiply_add_fusion.2 = f32[1,3,12,128]{3,1,2,0:T(4,128)S(1)} fusion(f32[1,3,12,128]{3,1,2,0:T(4,128)S(1)} %get-tuple-element.208, f32[1,3,16,128]{3,1,2,0:T(4,128)S(1)} %bitcast.159, f32[12,128]{1,0:T(8,128)S(1)} %get-tuple-element.207, f32[12,128]{1,0:T(8,128)S(1)} %get-tuple-element.180, f32[12,128,384]{2,1,0:T(8,128)S(1)} %get-tuple-element.181, ...), kind=kOutput, calls=%fused_computation.27.clone.1 | convolution fusion | flops 21284352 | bytes 2486784 | tf_op jit(solution)/shard_map/while/body/eval_jaxpr/...aun,...san->...sau/dot_general | solution.py:73
  57.9 0.6 gather_fusion.1
  58.6 2.3 %fusion.75 = (f32[8,128]{1,0:T(8,128)S(1)}, f32[8,128,384]{2,1,0:T(8,128)S(1)}) fusion(f32[3,8,384]{2,0,1:T(4,128)S(1)} %bitcast.162, pred[8,384]{1,0:T(8,128)(4,1)S(1)} %broadcast_bitcast_fusion.2, f32[1,3,12,128]{3,1,2,0:T(4,128)S(1)} %multiply_add_fusion.2, f32[8,384]{1,0:T(8,128)S(1)} %bitcast.170, f32[8,128]{1,0:T(8,128)S(1)} %multiply_reduce_fusion.11), kind=kOutput, calls=%fused_computation.107.clone.1 | convolution fusion | flops 16130048 | bytes 1661952 | tf_op jit(solution)/shard_map/while/body/eval_jaxpr/...euh,...euw->...uhw/dot_general | solution.py:66
  60.9 1.8 %fusion.77 = f32[1,3,1024]{2,1,0:T(4,128)S(1)} fusion(f32[8,128,384]{2,1,0:T(8,128)S(1)} %get-tuple-element.182, f32[3,8,384]{2,0,1:T(4,128)S(1)} %bitcast.163, pred[8,384]{1,0:T(8,128)(4,1)S(1)} %broadcast_bitcast_fusion.2, f32[1,3,8,128]{3,1,2,0:T(4,128)S(1)} %get-tuple-element.210, f32[1,3,12,128]{3,1,2,0:T(4,128)S(1)} %multiply_add_fusion.2, ...), kind=kOutput, calls=%fused_computation.13.clone.1 | convolution fusion | flops 14189568 | bytes 1657856 | tf_op jit(solution)/shard_map/while/body/eval_jaxpr/...aun,...san->...sau/dot_general | solution.py:73
  62.7 2.9 %collective-permute-start.1 = (f32[1,3,512]{2,1,0:T(4,128)S(1)}, f32[1,3,512]{2,1,0:T(4,128)S(1)}, u32[]{:S(2)}, u32[]{:S(2)}) collective-permute-start(f32[1,3,512]{2,1,0:T(4,128)S(1)} %get-tuple-element.179), channel_id=1, source_target_pairs={{1,0},{2,1},{3,2},{4,3},{5,4},{6,5},{7,6},{8,7},{9,8},{10,9},{11,1... | collective-permute-start | bytes 18440 | tf_op jit(solution)/shard_map/while/body/eval_jaxpr/ppermute | solution.py:30
  67.0 0.6 gather_fusion
  67.8 3.3 %fusion.74 = (f32[12,128]{1,0:T(8,128)S(1)}, f32[12,128,384]{2,1,0:T(8,128)S(1)}) fusion(f32[3,12,384]{2,0,1:T(4,128)S(1)} %bitcast.154, pred[12,384]{1,0:T(8,128)(4,1)S(1)} %bitcast.168, f32[1,3,16,128]{3,1,2,0:T(4,128)S(1)} %bitcast.158, f32[12,384]{1,0:T(8,128)S(1)} %bitcast.167, f32[12,128]{1,0:T(8,128)S(1)} %multiply_reduce_fusion.9), kind=kOutput, calls=%fused_computation.106.clone.1 | convolution fusion | flops 24195072 | bytes 2502656 | tf_op jit(solution)/shard_map/while/body/eval_jaxpr/...euh,...euw->...uhw/dot_general | solution.py:66
  71.1 2.6 %multiply_add_fusion.2 = f32[1,3,12,128]{3,1,2,0:T(4,128)S(1)} fusion(f32[1,3,12,128]{3,1,2,0:T(4,128)S(1)} %get-tuple-element.208, f32[1,3,16,128]{3,1,2,0:T(4,128)S(1)} %bitcast.159, f32[12,128]{1,0:T(8,128)S(1)} %get-tuple-element.207, f32[12,128]{1,0:T(8,128)S(1)} %get-tuple-element.180, f32[12,128,384]{2,1,0:T(8,128)S(1)} %get-tuple-element.181, ...), kind=kOutput, calls=%fused_computation.27.clone.1 | convolution fusion | flops 21284352 | bytes 2486784 | tf_op jit(solution)/shard_map/while/body/eval_jaxpr/...aun,...san->...sau/dot_general | solution.py:73
  73.8 0.6 gather_fusion.1
  74.5 2.3 %fusion.75 = (f32[8,128]{1,0:T(8,128)S(1)}, f32[8,128,384]{2,1,0:T(8,128)S(1)}) fusion(f32[3,8,384]{2,0,1:T(4,128)S(1)} %bitcast.162, pred[8,384]{1,0:T(8,128)(4,1)S(1)} %broadcast_bitcast_fusion.2, f32[1,3,12,128]{3,1,2,0:T(4,128)S(1)} %multiply_add_fusion.2, f32[8,384]{1,0:T(8,128)S(1)} %bitcast.170, f32[8,128]{1,0:T(8,128)S(1)} %multiply_reduce_fusion.11), kind=kOutput, calls=%fused_computation.107.clone.1 | convolution fusion | flops 16130048 | bytes 1661952 | tf_op jit(solution)/shard_map/while/body/eval_jaxpr/...euh,...euw->...uhw/dot_general | solution.py:66
  76.8 1.8 %fusion.77 = f32[1,3,1024]{2,1,0:T(4,128)S(1)} fusion(f32[8,128,384]{2,1,0:T(8,128)S(1)} %get-tuple-element.182, f32[3,8,384]{2,0,1:T(4,128)S(1)} %bitcast.163, pred[8,384]{1,0:T(8,128)(4,1)S(1)} %broadcast_bitcast_fusion.2, f32[1,3,8,128]{3,1,2,0:T(4,128)S(1)} %get-tuple-element.210, f32[1,3,12,128]{3,1,2,0:T(4,128)S(1)} %multiply_add_fusion.2, ...), kind=kOutput, calls=%fused_computation.13.clone.1 | convolution fusion | flops 14189568 | bytes 1657856 | tf_op jit(solution)/shard_map/while/body/eval_jaxpr/...aun,...san->...sau/dot_general | solution.py:73
  78.6 2.9 %collective-permute-start.1 = (f32[1,3,512]{2,1,0:T(4,128)S(1)}, f32[1,3,512]{2,1,0:T(4,128)S(1)}, u32[]{:S(2)}, u32[]{:S(2)}) collective-permute-start(f32[1,3,512]{2,1,0:T(4,128)S(1)} %get-tuple-element.179), channel_id=1, source_target_pairs={{1,0},{2,1},{3,2},{4,3},{5,4},{6,5},{7,6},{8,7},{9,8},{10,9},{11,1... | collective-permute-start | bytes 18440 | tf_op jit(solution)/shard_map/while/body/eval_jaxpr/ppermute | solution.py:30
  82.9 0.6 gather_fusion
  83.7 3.3 %fusion.74 = (f32[12,128]{1,0:T(8,128)S(1)}, f32[12,128,384]{2,1,0:T(8,128)S(1)}) fusion(f32[3,12,384]{2,0,1:T(4,128)S(1)} %bitcast.154, pred[12,384]{1,0:T(8,128)(4,1)S(1)} %bitcast.168, f32[1,3,16,128]{3,1,2,0:T(4,128)S(1)} %bitcast.158, f32[12,384]{1,0:T(8,128)S(1)} %bitcast.167, f32[12,128]{1,0:T(8,128)S(1)} %multiply_reduce_fusion.9), kind=kOutput, calls=%fused_computation.106.clone.1 | convolution fusion | flops 24195072 | bytes 2502656 | tf_op jit(solution)/shard_map/while/body/eval_jaxpr/...euh,...euw->...uhw/dot_general | solution.py:66
  87.0 2.6 %multiply_add_fusion.2 = f32[1,3,12,128]{3,1,2,0:T(4,128)S(1)} fusion(f32[1,3,12,128]{3,1,2,0:T(4,128)S(1)} %get-tuple-element.208, f32[1,3,16,128]{3,1,2,0:T(4,128)S(1)} %bitcast.159, f32[12,128]{1,0:T(8,128)S(1)} %get-tuple-element.207, f32[12,128]{1,0:T(8,128)S(1)} %get-tuple-element.180, f32[12,128,384]{2,1,0:T(8,128)S(1)} %get-tuple-element.181, ...), kind=kOutput, calls=%fused_computation.27.clone.1 | convolution fusion | flops 21284352 | bytes 2486784 | tf_op jit(solution)/shard_map/while/body/eval_jaxpr/...aun,...san->...sau/dot_general | solution.py:73
  89.7 0.6 gather_fusion.1
  90.4 2.3 %fusion.75 = (f32[8,128]{1,0:T(8,128)S(1)}, f32[8,128,384]{2,1,0:T(8,128)S(1)}) fusion(f32[3,8,384]{2,0,1:T(4,128)S(1)} %bitcast.162, pred[8,384]{1,0:T(8,128)(4,1)S(1)} %broadcast_bitcast_fusion.2, f32[1,3,12,128]{3,1,2,0:T(4,128)S(1)} %multiply_add_fusion.2, f32[8,384]{1,0:T(8,128)S(1)} %bitcast.170, f32[8,128]{1,0:T(8,128)S(1)} %multiply_reduce_fusion.11), kind=kOutput, calls=%fused_computation.107.clone.1 | convolution fusion | flops 16130048 | bytes 1661952 | tf_op jit(solution)/shard_map/while/body/eval_jaxpr/...euh,...euw->...uhw/dot_general | solution.py:66
  92.6 1.8 %fusion.77 = f32[1,3,1024]{2,1,0:T(4,128)S(1)} fusion(f32[8,128,384]{2,1,0:T(8,128)S(1)} %get-tuple-element.182, f32[3,8,384]{2,0,1:T(4,128)S(1)} %bitcast.163, pred[8,384]{1,0:T(8,128)(4,1)S(1)} %broadcast_bitcast_fusion.2, f32[1,3,8,128]{3,1,2,0:T(4,128)S(1)} %get-tuple-element.210, f32[1,3,12,128]{3,1,2,0:T(4,128)S(1)} %multiply_add_fusion.2, ...), kind=kOutput, calls=%fused_computation.13.clone.1 | convolution fusion | flops 14189568 | bytes 1657856 | tf_op jit(solution)/shard_map/while/body/eval_jaxpr/...aun,...san->...sau/dot_general | solution.py:73
  94.4 3.1 %collective-permute-start.4 = (f32[3,128]{1,0:T(4,128)S(1)}, f32[3,128]{1,0:T(4,128)S(1)}, u32[]{:S(2)}, u32[]{:S(2)}) collective-permute-start(f32[3,128]{1,0:T(4,128)S(1)} %slice_bitcast_fusion), channel_id=1, source_target_pairs={{0,32},{32,64},{64,96},{96,128},{128,160},{160,192},{192,224},{224... | collective-permute-start | bytes 4616 | tf_op jit(solution)/shard_map/ppermute | solution.py:40
  98.8 1.1 collective-permute-done.4
  99.9 0.6 fusion.36
  100.5 1.2 broadcast_in_dim.80
  101.8 9.5 %all-to-all-start = ((f32[32,1,1]{2,1,0:T(1,128)}), f32[32,1,1]{2,1,0:T(1,128)S(1)}, u32[]{:S(2)}, u32[]{:S(2)}) async-start(f32[32,1,1]{2,1,0:T(1,128)} %broadcast_in_dim.80), calls=%async_computation | async-start | bytes 32768 | tf_op jit(solution)/shard_map/all_to_all | solution.py:45
  111.3 5.2 %collective-permute-start.7 = (f32[1,3,1024]{2,1,0:T(4,128)S(1)}, f32[1,3,1024]{2,1,0:T(4,128)S(1)}, u32[]{:S(2)}, u32[]{:S(2)}) collective-permute-start(f32[1,3,1024]{2,1,0:T(4,128)S(1)} %get-tuple-element.44), channel_id=1, source_target_pairs={{0,32},{32,64},{64,96},{96,128},{128,160},{160,192},{192,224},{224... | collective-permute-start | bytes 36872 | tf_op jit(solution)/shard_map/ppermute | solution.py:28
  116.5 7.2 %all-to-all-done = f32[32,1,1]{2,1,0:T(1,128)S(1)} async-done(((f32[32,1,1]{2,1,0:T(1,128)}), f32[32,1,1]{2,1,0:T(1,128)S(1)}, u32[]{:S(2)}, u32[]{:S(2)}) %all-to-all-start) | async-done | bytes 160 | tf_op jit(solution)/shard_map/all_to_all | solution.py:45
  123.7 0.6 reduce_sum.95
  125.1 0.6 broadcast_in_dim.81
  125.7 7.2 %all-to-all-start.1 = ((f32[16,1,1]{2,1,0:T(1,128)}), f32[16,1,1]{2,1,0:T(1,128)S(1)}, u32[]{:S(2)}, u32[]{:S(2)}) async-start(f32[16,1,1]{2,1,0:T(1,128)} %broadcast_in_dim.81), calls=%async_computation.1 | async-start | bytes 16384 | tf_op jit(solution)/shard_map/all_to_all | solution.py:45
  132.8 2.8 %collective-permute-start.8 = (f32[1,3,1024]{2,1,0:T(4,128)S(1)}, f32[1,3,1024]{2,1,0:T(4,128)S(1)}, u32[]{:S(2)}, u32[]{:S(2)}) collective-permute-start(f32[1,3,1024]{2,1,0:T(4,128)S(1)} %get-tuple-element.44), channel_id=1, source_target_pairs={{32,0},{64,32},{96,64},{128,96},{160,128},{192,160},{224,192},{256... | collective-permute-start | bytes 36872 | tf_op jit(solution)/shard_map/ppermute | solution.py:30
  135.6 2.8 %all-to-all-done.1 = f32[16,1,1]{2,1,0:T(1,128)S(1)} async-done(((f32[16,1,1]{2,1,0:T(1,128)}), f32[16,1,1]{2,1,0:T(1,128)S(1)}, u32[]{:S(2)}, u32[]{:S(2)}) %all-to-all-start.1) | async-done | bytes 96 | tf_op jit(solution)/shard_map/all_to_all | solution.py:45
  138.4 0.5 constant_dynamic-slice_fusion
  138.9 4.0 %collective-permute-start.5 = (f32[1]{0:T(128)}, f32[1]{0:T(128)}, u32[]{:S(2)}, u32[]{:S(2)}) collective-permute-start(f32[1]{0:T(128)} %bitcast.9), channel_id=1, source_target_pairs={{0,32},{32,64},{64,96},{96,128},{128,160},{160,192},{192,224},{224... | collective-permute-start | bytes 20 | tf_op jit(solution)/shard_map/ppermute | solution.py:28
  142.9 1.9 %collective-permute-start.6 = (f32[1]{0:T(128)}, f32[1]{0:T(128)}, u32[]{:S(2)}, u32[]{:S(2)}) collective-permute-start(f32[1]{0:T(128)} %bitcast.9), channel_id=1, source_target_pairs={{32,0},{64,32},{96,64},{128,96},{160,128},{192,160},{224,192},{256... | collective-permute-start | bytes 20 | tf_op jit(solution)/shard_map/ppermute | solution.py:30
  146.8 3.8 %collective-permute-done.6 = f32[1]{0:T(128)} collective-permute-done((f32[1]{0:T(128)}, f32[1]{0:T(128)}, u32[]{:S(2)}, u32[]{:S(2)}) %collective-permute-start.6) | collective-permute-done | bytes 36 | tf_op jit(solution)/shard_map/ppermute | solution.py:30
  150.5 2.7 %fusion.40 = (f32[]{:T(128)}, f32[]{:T(128)}) fusion(s32[]{:T(128)} %bitcast.13, s32[]{:T(128)} %bitcast.1, f32[1,1]{1,0:T(1,128)} %bitcast.11, f32[1,1]{1,0:T(1,128)} %get-tuple-element.127, f32[1,1]{1,0:T(1,128)} %bitcast.10), kind=kLoop, calls=%fused_computation.89 | loop fusion | flops 22 | bytes 28 | tf_op jit(solution)/shard_map/reduce_sum | solution.py:153
  155.4 0.6 dot_general.22
  (174 shorter events, 7.9 us)
Async XLA Ops:
  1.3 12.9 %collective-permute-start.2 = (f32[1,3,512]{2,0,1:T(1,128)S(1)}, f32[1,3,512]{2,0,1:T(1,128)S(1)}, u32[]{:S(2)}, u32[]{:S(2)}) collective-permute-start(f32[1,3,512]{2,0,1:T(1,128)S(1)} %get-tuple-element.125), channel_id=1, source_target_pairs={{0,1},{1,2},{2,3},{3,4},{4,5},{5,6},{6,7},{7,8},{8,9},{9,10},{10,1... | collective-permute-start | bytes 18440 | tf_op jit(solution)/shard_map/ppermute | solution.py:28
  1.3 12.9 %collective-permute-start.3 = (f32[1,3,512]{2,0,1:T(1,128)S(1)}, f32[1,3,512]{2,0,1:T(1,128)S(1)}, u32[]{:S(2)}, u32[]{:S(2)}) collective-permute-start(f32[1,3,512]{2,0,1:T(1,128)S(1)} %get-tuple-element.126), channel_id=1, source_target_pairs={{1,0},{2,1},{3,2},{4,3},{5,4},{6,5},{7,6},{8,7},{9,8},{10,9},{11,1... | collective-permute-start | bytes 18440 | tf_op jit(solution)/shard_map/ppermute | solution.py:30
  15.0 4.3 %collective-permute-start = (f32[1,3,512]{2,1,0:T(4,128)S(1)}, f32[1,3,512]{2,1,0:T(4,128)S(1)}, u32[]{:S(2)}, u32[]{:S(2)}) collective-permute-start(f32[1,3,512]{2,1,0:T(4,128)S(1)} %get-tuple-element.178), channel_id=1, source_target_pairs={{0,1},{1,2},{2,3},{3,4},{4,5},{5,6},{6,7},{7,8},{8,9},{9,10},{10,1... | collective-permute-start | bytes 18440 | tf_op jit(solution)/shard_map/while/body/eval_jaxpr/ppermute | solution.py:28
  15.1 4.3 %collective-permute-start.1 = (f32[1,3,512]{2,1,0:T(4,128)S(1)}, f32[1,3,512]{2,1,0:T(4,128)S(1)}, u32[]{:S(2)}, u32[]{:S(2)}) collective-permute-start(f32[1,3,512]{2,1,0:T(4,128)S(1)} %get-tuple-element.179), channel_id=1, source_target_pairs={{1,0},{2,1},{3,2},{4,3},{5,4},{6,5},{7,6},{8,7},{9,8},{10,9},{11,1... | collective-permute-start | bytes 18440 | tf_op jit(solution)/shard_map/while/body/eval_jaxpr/ppermute | solution.py:30
  30.9 4.3 %collective-permute-start = (f32[1,3,512]{2,1,0:T(4,128)S(1)}, f32[1,3,512]{2,1,0:T(4,128)S(1)}, u32[]{:S(2)}, u32[]{:S(2)}) collective-permute-start(f32[1,3,512]{2,1,0:T(4,128)S(1)} %get-tuple-element.178), channel_id=1, source_target_pairs={{0,1},{1,2},{2,3},{3,4},{4,5},{5,6},{6,7},{7,8},{8,9},{9,10},{10,1... | collective-permute-start | bytes 18440 | tf_op jit(solution)/shard_map/while/body/eval_jaxpr/ppermute | solution.py:28
  30.9 4.3 %collective-permute-start.1 = (f32[1,3,512]{2,1,0:T(4,128)S(1)}, f32[1,3,512]{2,1,0:T(4,128)S(1)}, u32[]{:S(2)}, u32[]{:S(2)}) collective-permute-start(f32[1,3,512]{2,1,0:T(4,128)S(1)} %get-tuple-element.179), channel_id=1, source_target_pairs={{1,0},{2,1},{3,2},{4,3},{5,4},{6,5},{7,6},{8,7},{9,8},{10,9},{11,1... | collective-permute-start | bytes 18440 | tf_op jit(solution)/shard_map/while/body/eval_jaxpr/ppermute | solution.py:30
  46.8 4.3 %collective-permute-start = (f32[1,3,512]{2,1,0:T(4,128)S(1)}, f32[1,3,512]{2,1,0:T(4,128)S(1)}, u32[]{:S(2)}, u32[]{:S(2)}) collective-permute-start(f32[1,3,512]{2,1,0:T(4,128)S(1)} %get-tuple-element.178), channel_id=1, source_target_pairs={{0,1},{1,2},{2,3},{3,4},{4,5},{5,6},{6,7},{7,8},{8,9},{9,10},{10,1... | collective-permute-start | bytes 18440 | tf_op jit(solution)/shard_map/while/body/eval_jaxpr/ppermute | solution.py:28
  46.8 4.3 %collective-permute-start.1 = (f32[1,3,512]{2,1,0:T(4,128)S(1)}, f32[1,3,512]{2,1,0:T(4,128)S(1)}, u32[]{:S(2)}, u32[]{:S(2)}) collective-permute-start(f32[1,3,512]{2,1,0:T(4,128)S(1)} %get-tuple-element.179), channel_id=1, source_target_pairs={{1,0},{2,1},{3,2},{4,3},{5,4},{6,5},{7,6},{8,7},{9,8},{10,9},{11,1... | collective-permute-start | bytes 18440 | tf_op jit(solution)/shard_map/while/body/eval_jaxpr/ppermute | solution.py:30
  62.7 4.3 %collective-permute-start = (f32[1,3,512]{2,1,0:T(4,128)S(1)}, f32[1,3,512]{2,1,0:T(4,128)S(1)}, u32[]{:S(2)}, u32[]{:S(2)}) collective-permute-start(f32[1,3,512]{2,1,0:T(4,128)S(1)} %get-tuple-element.178), channel_id=1, source_target_pairs={{0,1},{1,2},{2,3},{3,4},{4,5},{5,6},{6,7},{7,8},{8,9},{9,10},{10,1... | collective-permute-start | bytes 18440 | tf_op jit(solution)/shard_map/while/body/eval_jaxpr/ppermute | solution.py:28
  62.7 4.3 %collective-permute-start.1 = (f32[1,3,512]{2,1,0:T(4,128)S(1)}, f32[1,3,512]{2,1,0:T(4,128)S(1)}, u32[]{:S(2)}, u32[]{:S(2)}) collective-permute-start(f32[1,3,512]{2,1,0:T(4,128)S(1)} %get-tuple-element.179), channel_id=1, source_target_pairs={{1,0},{2,1},{3,2},{4,3},{5,4},{6,5},{7,6},{8,7},{9,8},{10,9},{11,1... | collective-permute-start | bytes 18440 | tf_op jit(solution)/shard_map/while/body/eval_jaxpr/ppermute | solution.py:30
  78.6 4.3 %collective-permute-start = (f32[1,3,512]{2,1,0:T(4,128)S(1)}, f32[1,3,512]{2,1,0:T(4,128)S(1)}, u32[]{:S(2)}, u32[]{:S(2)}) collective-permute-start(f32[1,3,512]{2,1,0:T(4,128)S(1)} %get-tuple-element.178), channel_id=1, source_target_pairs={{0,1},{1,2},{2,3},{3,4},{4,5},{5,6},{6,7},{7,8},{8,9},{9,10},{10,1... | collective-permute-start | bytes 18440 | tf_op jit(solution)/shard_map/while/body/eval_jaxpr/ppermute | solution.py:28
  78.6 4.3 %collective-permute-start.1 = (f32[1,3,512]{2,1,0:T(4,128)S(1)}, f32[1,3,512]{2,1,0:T(4,128)S(1)}, u32[]{:S(2)}, u32[]{:S(2)}) collective-permute-start(f32[1,3,512]{2,1,0:T(4,128)S(1)} %get-tuple-element.179), channel_id=1, source_target_pairs={{1,0},{2,1},{3,2},{4,3},{5,4},{6,5},{7,6},{8,7},{9,8},{10,9},{11,1... | collective-permute-start | bytes 18440 | tf_op jit(solution)/shard_map/while/body/eval_jaxpr/ppermute | solution.py:30
  94.4 5.5 %collective-permute-start.4 = (f32[3,128]{1,0:T(4,128)S(1)}, f32[3,128]{1,0:T(4,128)S(1)}, u32[]{:S(2)}, u32[]{:S(2)}) collective-permute-start(f32[3,128]{1,0:T(4,128)S(1)} %slice_bitcast_fusion), channel_id=1, source_target_pairs={{0,32},{32,64},{64,96},{96,128},{128,160},{160,192},{192,224},{224... | collective-permute-start | bytes 4616 | tf_op jit(solution)/shard_map/ppermute | solution.py:40
  101.8 21.9 %all-to-all-start = ((f32[32,1,1]{2,1,0:T(1,128)}), f32[32,1,1]{2,1,0:T(1,128)S(1)}, u32[]{:S(2)}, u32[]{:S(2)}) async-start(f32[32,1,1]{2,1,0:T(1,128)} %broadcast_in_dim.80), calls=%async_computation | async-start | bytes 32768 | tf_op jit(solution)/shard_map/all_to_all | solution.py:45
  111.3 43.8 %collective-permute-start.7 = (f32[1,3,1024]{2,1,0:T(4,128)S(1)}, f32[1,3,1024]{2,1,0:T(4,128)S(1)}, u32[]{:S(2)}, u32[]{:S(2)}) collective-permute-start(f32[1,3,1024]{2,1,0:T(4,128)S(1)} %get-tuple-element.44), channel_id=1, source_target_pairs={{0,32},{32,64},{64,96},{96,128},{128,160},{160,192},{192,224},{224... | collective-permute-start | bytes 36872 | tf_op jit(solution)/shard_map/ppermute | solution.py:28
  125.7 12.7 %all-to-all-start.1 = ((f32[16,1,1]{2,1,0:T(1,128)}), f32[16,1,1]{2,1,0:T(1,128)S(1)}, u32[]{:S(2)}, u32[]{:S(2)}) async-start(f32[16,1,1]{2,1,0:T(1,128)} %broadcast_in_dim.81), calls=%async_computation.1 | async-start | bytes 16384 | tf_op jit(solution)/shard_map/all_to_all | solution.py:45
  132.8 22.3 %collective-permute-start.8 = (f32[1,3,1024]{2,1,0:T(4,128)S(1)}, f32[1,3,1024]{2,1,0:T(4,128)S(1)}, u32[]{:S(2)}, u32[]{:S(2)}) collective-permute-start(f32[1,3,1024]{2,1,0:T(4,128)S(1)} %get-tuple-element.44), channel_id=1, source_target_pairs={{32,0},{64,32},{96,64},{128,96},{160,128},{192,160},{224,192},{256... | collective-permute-start | bytes 36872 | tf_op jit(solution)/shard_map/ppermute | solution.py:30
  138.9 7.8 %collective-permute-start.5 = (f32[1]{0:T(128)}, f32[1]{0:T(128)}, u32[]{:S(2)}, u32[]{:S(2)}) collective-permute-start(f32[1]{0:T(128)} %bitcast.9), channel_id=1, source_target_pairs={{0,32},{32,64},{64,96},{96,128},{128,160},{160,192},{192,224},{224... | collective-permute-start | bytes 20 | tf_op jit(solution)/shard_map/ppermute | solution.py:28
  142.9 7.6 %collective-permute-start.6 = (f32[1]{0:T(128)}, f32[1]{0:T(128)}, u32[]{:S(2)}, u32[]{:S(2)}) collective-permute-start(f32[1]{0:T(128)} %bitcast.9), channel_id=1, source_target_pairs={{32,0},{64,32},{96,64},{128,96},{160,128},{192,160},{224,192},{256... | collective-permute-start | bytes 20 | tf_op jit(solution)/shard_map/ppermute | solution.py:30
where the time goes:
time: 158 us; the launch traced here: 157 us
  starting transfers between devices  57.3 us (36%)
  matrix products  50 us (32%)
  waiting for transfers between devices  17.5 us (11%)
  local copies, waits for them, and re-layouts  17.3 us (11%)
  between operations  7.74 us (5%)
  other arithmetic  6.61 us (4%)
    ppermute x8, starting transfers between devices, extended(): lax.ppermute(head, axis, [((i + 1) % count, i) for i in range(ends)])  28.3 us
    dot_general x10, matrix products, pair_forces(): jnp.einsum('...euh,...euw->...uhw', swarm_centres, partner_beads, precisi...  27.8 us
    dot_general x10, matrix products, pair_forces(): jnp.einsum('...aun,...san->...sau', weight_factors, partner_beads, precis...  22 us
    all_to_all x2, starting transfers between devices, from_everyone(): return lax.all_to_all(copies, axis, split_axis=0, concat_axis=0, tiled=True)  16.7 us
    all_to_all x2, waiting for transfers between devices, from_everyone(): return lax.all_to_all(copies, axis, split_axis=0, concat_axis=0, tiled=True)  10 us
    ppermute x8, starting transfers between devices, extended(): lax.ppermute(tail, axis, [(i, (i + 1) % count) for i in range(ends)])  9.21 us
    gather x10, local copies, waits for them, and re-layouts, block_forces(): partners = jnp.take(widened, partner_rows, axis=-2)  6.03 us
    ppermute x8, waiting for transfers between devices, extended(): lax.ppermute(head, axis, [((i + 1) % count, i) for i in range(ends)])  3.9 us
  transfers between devices with their start and end apart: 19, of which 9 were waited for; matrix products, arithmetic and copies ran while one was open for 8% of the time, Pallas kernels for 0%

commit v1 on v0

v1 whole, which is shorter than its diff:
```python
import functools
import math

import jax
import jax.numpy as jnp
from jax import lax
from jax.experimental import pallas as pl
from jax.experimental.pallas import tpu as pltpu
from jax.sharding import PartitionSpec as P

MESH = pl.DeviceIdType.MESH
F32, BF16 = jnp.float32, jnp.bfloat16

BLOCK = 128
HALO = 2
NB = 8
NEIGHBOURS = 3
IMAGES = 16
N_SPACE = 32
BLOCKS = NB * N_SPACE
TIME_STEP = 0.05
RESTRAINT = 1.0
COUPLING = 3.0
KERNEL_RATE = 0.125
EPSILON = 1e-06
CODE_SCALE = 65536.0

ROUNDS = (4, 3, 3)
OWN = NB
EXT = 3 * NB

SCALE = math.sqrt(KERNEL_RATE * math.log2(math.e))
PULL = TIME_STEP * COUPLING / (NEIGHBOURS * BLOCK)
PARTS = 32


def dot(a, b):
    return lax.dot_general(a, b, (((1,), (0,)), ((), ())), preferred_element_type=F32)


def split3(v):
    high = v.astype(BF16).astype(F32)
    rest = v - high
    middle = rest.astype(BF16).astype(F32)
    return high, middle, rest - middle


def operands(y):
    row = lax.broadcasted_iota(jnp.int32, y.shape, 1)
    y = jnp.where(row < 3, y, 0.0)
    square = jnp.sum(y * y, axis=1, keepdims=True)
    partner = jnp.where(row == 3, square, jnp.where(row == 4, 1.0, y))
    centre = jnp.where(row == 3, -1.0, jnp.where(row == 4, -square, y + y))
    ph, pm, plow = split3(partner)
    ch, cm, cl = split3(centre)
    a = jnp.concatenate([ph, ph, ph, pm, pm, plow], axis=1)
    b = jnp.concatenate([ch, cm, cl, ch, cm, ch], axis=1).astype(BF16)
    x = jnp.concatenate([ph, pm, plow, jnp.zeros_like(y)], axis=1).astype(BF16)
    return a, b, x


def kernel(x_ref, table, bracket, code, out_ref, fraction_ref, cur, anchor, aop, bop, xop, raw, got, around, plane, mine, part, parts, sems):
    image, slab = lax.axis_index("image"), lax.axis_index("space")

    def beside(d):
        return (image, lax.rem(slab + d + N_SPACE, N_SPACE))

    def across(d):
        return (lax.rem(image + d + IMAGES, IMAGES), slab)

    barrier = pltpu.get_barrier_semaphore()

    def greet_beside(d, _):
        pl.semaphore_signal(barrier, inc=1, device_id=beside(d), device_id_type=MESH)
        return 0

    def greet_across(d, _):
        pl.semaphore_signal(barrier, inc=1, device_id=across(d), device_id_type=MESH)
        return 0

    lax.fori_loop(1, N_SPACE, greet_beside, 0)
    lax.fori_loop(1, IMAGES, greet_across, 0)

    def store_operands(lo, y):
        a, b, x = operands(y)
        n = y.shape[0]
        bop[lo : lo + n] = b
        xop[lo : lo + n] = x
        for i in range(n):
            aop[lo + i] = a[i].T.astype(BF16)

    def take_slab(lo, slab_ref, scale):
        pad = jnp.zeros((NB, 5, BLOCK), F32)
        rows = [slab_ref[c].reshape(NB, 1, BLOCK) for c in range(3)]
        y = jnp.concatenate(rows + [pad], axis=1) * scale
        cur[lo : lo + NB] = y
        store_operands(lo, y)
        return y

    def exchange(r, source):
        copies = []
        for side, d in enumerate((1, -1)):
            copies.append(
                pltpu.make_async_remote_copy(
                    src_ref=source,
                    dst_ref=got.at[r, side],
                    send_sem=sems.at[0, 2 * r + side],
                    recv_sem=sems.at[1, 2 * r + side],
                    device_id=beside(d),
                    device_id_type=MESH,
                )
            )
        return copies

    own = take_slab(OWN, x_ref, SCALE)
    anchor[1] = own[0]
    pl.semaphore_wait(barrier, N_SPACE - 1 + IMAGES - 1)

    def step(lo, n):
        blocks = range(lo, lo + n)
        first = slab * NB + BLOCKS - OWN
        partners = [
            [e - HALO + table[k, lax.rem(first + e, BLOCKS)] for k in range(NEIGHBOURS)]
            for e in blocks
        ]
        weights = []
        for e, ps in zip(blocks, partners):
            exponent = dot(jnp.concatenate([aop[p] for p in ps], axis=0), bop[e])
            w = jnp.exp2(exponent)
            high = w.astype(BF16)
            weights.append(jnp.concatenate([high, (w - high.astype(F32)).astype(BF16)], axis=0))
        sums = []
        for ps, w in zip(partners, weights):
            x = jnp.concatenate([xop[p] for p in ps], axis=1)
            total = dot(jnp.concatenate([x, x], axis=1), w)
            sums.append(total[0:8] + total[8:16] + total[16:24])
        y = cur[lo : lo + n]
        total = jnp.stack(sums, axis=0)
        y_new = y + PULL * (y * total[:, 4:5] - total)
        held = [
            y_new[i : i + 1] - (TIME_STEP * RESTRAINT) * (y[i : i + 1] - anchor[e // NB][None])
            if e % NB == 0
            else y_new[i : i + 1]
            for i, e in enumerate(blocks)
        ]
        y_new = jnp.concatenate(held, axis=0)
        cur[lo : lo + n] = y_new
        return y_new

    def steps(count):
        for t in range(count):
            reach = HALO * (count - 1 - t)
            lo, n = OWN - reach, NB + 2 * reach
            y = step(lo, n)
            if t < count - 1:
                store_operands(lo, y)
        return y

    def pack(ref, y):
        for c in range(3):
            ref[c] = y[:, c]

    copies = exchange(0, x_ref)
    for c in copies:
        c.start()
    for c in copies:
        c.wait()
    anchor[0] = take_slab(0, got.at[0, 0], SCALE)[0]
    anchor[2] = take_slab(2 * NB, got.at[0, 1], SCALE)[0]
    y = steps(ROUNDS[0])
    for r in range(1, len(ROUNDS)):
        pack(raw.at[r], y)
        copies = exchange(r, raw.at[r])
        for c in copies:
            c.start()
        store_operands(OWN, y)
        for c in copies:
            c.wait()
        take_slab(0, got.at[r, 0], 1.0)
        take_slab(2 * NB, got.at[r, 1], 1.0)
        y = steps(ROUNDS[r])

    row = lax.broadcasted_iota(jnp.int32, (8, BLOCK), 0)
    mine[...] = jnp.where(row < 3, y[0], 0.0)[0:4]

    def send_protein(d, _):
        pltpu.make_async_remote_copy(
            src_ref=mine, dst_ref=plane.at[image], send_sem=sems.at[0, 6], recv_sem=sems.at[1, 6],
            device_id=across(d), device_id_type=MESH,
        ).start()
        return 0

    lax.fori_loop(1, IMAGES, send_protein, 0)
    pack(raw.at[0], y)
    images = [
        pltpu.make_async_remote_copy(
            src_ref=raw.at[0], dst_ref=around.at[side], send_sem=sems.at[0, 7 + side], recv_sem=sems.at[1, 7 + side],
            device_id=across(d), device_id_type=MESH,
        )
        for side, d in enumerate((1, -1))
    ]
    for c in images:
        c.start()
    others = plane.at[pl.ds(1, IMAGES - 1)]
    pltpu.make_async_copy(others, others, sems.at[1, 6]).wait()
    plane[image] = mine[...]

    every = plane[...]
    change = every[1:] - every[:-1]
    change = jnp.concatenate([jnp.zeros((1, 4, BLOCK), F32), change], axis=0)
    squares = jnp.sum(jnp.sum(change * change, axis=1), axis=1, keepdims=True)
    at_row = lax.broadcasted_iota(jnp.int32, (IMAGES, BLOCK), 0)
    at_lane = lax.broadcasted_iota(jnp.int32, (IMAGES, BLOCK), 1)
    part[...] = jnp.sum(jnp.where(at_row == at_lane, squares, 0.0), axis=0, keepdims=True)

    def send_part(d, _):
        pltpu.make_async_remote_copy(
            src_ref=part, dst_ref=parts.at[slab], send_sem=sems.at[0, 9], recv_sem=sems.at[1, 9],
            device_id=beside(d), device_id_type=MESH,
        ).start()
        return 0

    lax.fori_loop(1, N_SPACE, send_part, 0)
    for c in images:
        c.wait()
    pltpu.make_async_copy(others, others, sems.at[0, 6]).wait()
    rest = parts.at[pl.ds(1, N_SPACE - 1)]
    pltpu.make_async_copy(rest, rest, sems.at[1, 9]).wait()
    parts[slab] = part[...]

    lane = lax.broadcasted_iota(jnp.int32, (1, BLOCK), 1)
    total = jnp.sum(parts[...], axis=0)
    lengths = jnp.sqrt(total * (1.0 / SCALE**2) + EPSILON)
    lengths = jnp.where((lane > 0) & (lane < IMAGES), lengths, 0.0)

    def arc(k):
        return jnp.sum(jnp.where(lane <= k, lengths, 0.0), axis=1, keepdims=True)

    lower = bracket[0]
    full = arc(IMAGES - 1)
    arc_lower = arc(lower)
    place = jnp.full((1, 1), lower, jnp.int32).astype(F32) + jnp.full((1, 1), code[0], jnp.int32).astype(F32) / CODE_SCALE
    weight = (place / (IMAGES - 1) * full - arc_lower) / (arc(lower + 1) - arc_lower)
    fraction_ref[...] = jnp.broadcast_to(arc(image) / full, (1, BLOCK))
    earlier = lower < image
    for c in range(3):
        here = raw[0, c]
        below = jnp.where(earlier, around[0, c], here)
        above = jnp.where(earlier, here, around[1, c])
        out_ref[c] = ((1.0 - weight) * below + weight * above) * (1.0 / SCALE)
    pltpu.make_async_copy(rest, rest, sems.at[0, 9]).wait()


def body(positions, neighbours, brackets, codes):
    vmem, smem = (pl.BlockSpec(memory_space=s) for s in (pltpu.VMEM, pltpu.SMEM))
    rounds = len(ROUNDS)
    out, fraction = pl.pallas_call(
        kernel,
        out_shape=(jax.ShapeDtypeStruct((3, NB, BLOCK), F32), jax.ShapeDtypeStruct((1, BLOCK), F32)),
        in_specs=[vmem, smem, smem, smem],
        out_specs=(vmem, vmem),
        scratch_shapes=[
            pltpu.VMEM((EXT, 8, BLOCK), F32),
            pltpu.VMEM((3, 8, BLOCK), F32),
            pltpu.VMEM((EXT, BLOCK, 48), BF16),
            pltpu.VMEM((EXT, 48, BLOCK), BF16),
            pltpu.VMEM((EXT, 32, BLOCK), BF16),
            pltpu.VMEM((rounds, 3, NB, BLOCK), F32),
            pltpu.VMEM((rounds, 2, 3, NB, BLOCK), F32),
            pltpu.VMEM((2, 3, NB, BLOCK), F32),
            pltpu.VMEM((IMAGES, 4, BLOCK), F32),
            pltpu.VMEM((4, BLOCK), F32),
            pltpu.VMEM((1, BLOCK), F32),
            pltpu.VMEM((N_SPACE, 1, BLOCK), F32),
            pltpu.SemaphoreType.DMA((2, 10)),
        ],
        compiler_params=pltpu.CompilerParams(collective_id=0, has_side_effects=True, vmem_limit_bytes=48 << 20),
    )(positions.reshape(3, NB, BLOCK), neighbours.T, brackets, codes)
    return out.reshape(1, 3, NB * BLOCK), fraction[0, :1]


def solution(mesh):
    placed = (P("image", None, "space"), P(), P("image"), P("image"))
    return jax.shard_map(
        body,
        mesh=mesh,
        in_specs=placed,
        out_specs=(P("image", None, "space"), P("image")),
        check_vma=False,
    )
```

time: 158 us -> 54.2 us (0.34)
  the two profiles are of different devices: /device:TPU:24 before, /device:TPU:1 now
where the time goes in v1:
time: 54.2 us; the launch traced here: 54 us
  Pallas kernels  49.5 us (91%)
  between operations  3.13 us (6%)
  local copies, waits for them, and re-layouts  1.31 us (2%)
    pallas_call x1, Pallas kernels, body(): pl.pallas_call(kernel, out_shape=(jax.ShapeDtypeStruct((3, NB, BLOCK), F3...  49.5 us
    unnamed x5, local copies, waits for them, and re-layouts  1.31 us

profile of v1, /device:TPU:1, one launch (start us, length us, event | category | flops | bytes accessed | tf_op | source)
XLA Modules:
  0.0 54.0 jit_solution(17351946001653140770)
XLA Ops:
  0.6 0.0 copy-start.1
  1.9 0.0 copy-done.1
  2.0 0.0 copy-start
  2.0 0.7 %copy-done = f32[1,3,1024]{2,0,1:T(1,128)S(1)} copy-done((f32[1,3,1024]{2,0,1:T(1,128)S(1)}, f32[1,3,1024]{2,0,1:T(1,128)}, u32[]{:S(2)}) %copy-start) | copy-done | bytes 12312
  2.7 49.5 %shard_map.59 = (f32[3,8,128]{2,1,0:T(8,128)S(1)}, f32[1,128]{1,0:T(1,128)S(1)}) custom-call(f32[3,8,128]{2,1,0:T(8,128)S(1)} %bitcast.6, s32[3,256]{1,0:T(4,128)S(1)} %bitcast.7, s32[1]{0:T(128)S(6)} %copy.10.bracket, s32[1]{0:T(128)S(6)} %copy.11.code), custom_call_target="tpu_custom_call" | custom-call | tf_op jit(solution)/shard_map/pallas_call | solution.py:257
  52.2 0.6 %copy.12 = f32[1,3,1024]{2,0,1:T(1,128)} copy(f32[1,3,1024]{2,0,1:T(1,128)S(1)} %bitcast.5) | data formatting | bytes 24576
Async XLA Ops:
  0.6 1.3 %copy-start.1 = (s32[256,3]{0,1:T(4,128)S(1)}, s32[256,3]{0,1:T(4,128)}, u32[]{:S(2)}) copy-start(s32[256,3]{0,1:T(4,128)} %param.5) | copy-start | bytes 9220
  2.0 0.7 %copy-start = (f32[1,3,1024]{2,0,1:T(1,128)S(1)}, f32[1,3,1024]{2,0,1:T(1,128)}, u32[]{:S(2)}) copy-start(f32[1,3,1024]{2,0,1:T(1,128)} %param.4) | copy-start | bytes 36868

commit v2 on v1

--- a/solution.py
+++ b/solution.py
@@ -59,7 +59,10 @@
     return a, b, x
 
 
-def kernel(x_ref, table, bracket, code, out_ref, fraction_ref, cur, anchor, aop, bop, xop, raw, got, around, plane, mine, part, parts, sems):
+def kernel(
+    x_ref, table_in, images_ref, total_ref,
+    table, local_sem, relay_sems, cur, anchor, aop, bop, xop, raw, got, around, plane, mine, part, parts, sems,
+):
     image, slab = lax.axis_index("image"), lax.axis_index("space")
 
     def beside(d):
@@ -68,18 +71,38 @@
     def across(d):
         return (lax.rem(image + d + IMAGES, IMAGES), slab)
 
+    ring = sorted(range(1, N_SPACE), key=lambda d: -min(d, N_SPACE - d))
+    square = [(dx, dy) for dx in range(4) for dy in range(4) if (dx, dy) != (0, 0)]
+    square.sort(key=lambda d: -sum(min(v, 4 - v) for v in d))
+
+    def in_plane(d):
+        return (lax.rem(image // 4 + d[0], 4) * 4 + lax.rem(lax.rem(image, 4) + d[1], 4), slab)
+
+    def greet(semaphore, peers):
+        for peer in peers:
+            pl.semaphore_signal(semaphore, inc=1, device_id=peer, device_id_type=MESH)
+
     barrier = pltpu.get_barrier_semaphore()
-
-    def greet_beside(d, _):
-        pl.semaphore_signal(barrier, inc=1, device_id=beside(d), device_id_type=MESH)
-        return 0
-
-    def greet_across(d, _):
-        pl.semaphore_signal(barrier, inc=1, device_id=across(d), device_id_type=MESH)
-        return 0
-
-    lax.fori_loop(1, N_SPACE, greet_beside, 0)
-    lax.fori_loop(1, IMAGES, greet_across, 0)
+    near = [beside(1), beside(-1), across(1), across(-1)]
+    stages = [
+        [peer for far in reach for peer in far]
+        for reach in (
+            [(beside(1), beside(-1)), (across(1), across(-1))],
+            [(beside(2), beside(-2)), (across(2), across(-2))],
+            [(beside(4), beside(-4)), (across(4), across(-4))],
+            [(beside(8), beside(-8))],
+        )
+    ]
+
+    def relay(j):
+        if j > 0:
+            pl.semaphore_wait(relay_sems.at[j - 1], len(stages[j - 1]))
+        if j < len(stages):
+            greet(relay_sems.at[j], stages[j])
+
+    greet(barrier, near)
+    load = pltpu.make_async_copy(table_in, table, local_sem)
+    load.start()
 
     def store_operands(lo, y):
         a, b, x = operands(y)
@@ -112,9 +135,14 @@
             )
         return copies
 
+    pl.semaphore_wait(barrier, len(near))
+    copies = exchange(0, x_ref)
+    for c in copies:
+        c.start()
+    relay(0)
     own = take_slab(OWN, x_ref, SCALE)
     anchor[1] = own[0]
-    pl.semaphore_wait(barrier, N_SPACE - 1 + IMAGES - 1)
+    load.wait()
 
     def step(lo, n):
         blocks = range(lo, lo + n)
@@ -147,27 +175,27 @@
         cur[lo : lo + n] = y_new
         return y_new
 
-    def steps(count):
-        for t in range(count):
+    def steps(count, last, between):
+        for t in range(count - last):
             reach = HALO * (count - 1 - t)
             lo, n = OWN - reach, NB + 2 * reach
             y = step(lo, n)
             if t < count - 1:
                 store_operands(lo, y)
+            if t in between:
+                relay(between[t])
         return y
 
     def pack(ref, y):
         for c in range(3):
             ref[c] = y[:, c]
 
-    copies = exchange(0, x_ref)
-    for c in copies:
-        c.start()
     for c in copies:
         c.wait()
+    relay(1)
     anchor[0] = take_slab(0, got.at[0, 0], SCALE)[0]
     anchor[2] = take_slab(2 * NB, got.at[0, 1], SCALE)[0]
-    y = steps(ROUNDS[0])
+    y = steps(ROUNDS[0], 0, {1: 2})
     for r in range(1, len(ROUNDS)):
         pack(raw.at[r], y)
         copies = exchange(r, raw.at[r])
@@ -178,20 +206,20 @@
             c.wait()
         take_slab(0, got.at[r, 0], 1.0)
         take_slab(2 * NB, got.at[r, 1], 1.0)
-        y = steps(ROUNDS[r])
+        if r == 1:
+            relay(3)
+        y = steps(ROUNDS[r], int(r == len(ROUNDS) - 1), {})
+    relay(4)
 
     row = lax.broadcasted_iota(jnp.int32, (8, BLOCK), 0)
-    mine[...] = jnp.where(row < 3, y[0], 0.0)[0:4]
-
-    def send_protein(d, _):
+    head = step(OWN, 1)
+    mine[...] = jnp.where(row < 3, head[0], 0.0)[0:4]
+    for d in square:
         pltpu.make_async_remote_copy(
             src_ref=mine, dst_ref=plane.at[image], send_sem=sems.at[0, 6], recv_sem=sems.at[1, 6],
-            device_id=across(d), device_id_type=MESH,
+            device_id=in_plane(d), device_id_type=MESH,
         ).start()
-        return 0
-
-    lax.fori_loop(1, IMAGES, send_protein, 0)
-    pack(raw.at[0], y)
+    pack(raw.at[0], jnp.concatenate([head, step(OWN + 1, NB - 1)], axis=0))
     images = [
         pltpu.make_async_remote_copy(
             src_ref=raw.at[0], dst_ref=around.at[side], send_sem=sems.at[0, 7 + side], recv_sem=sems.at[1, 7 + side],
@@ -213,14 +241,11 @@
     at_lane = lax.broadcasted_iota(jnp.int32, (IMAGES, BLOCK), 1)
     part[...] = jnp.sum(jnp.where(at_row == at_lane, squares, 0.0), axis=0, keepdims=True)
 
-    def send_part(d, _):
+    for d in ring:
         pltpu.make_async_remote_copy(
             src_ref=part, dst_ref=parts.at[slab], send_sem=sems.at[0, 9], recv_sem=sems.at[1, 9],
             device_id=beside(d), device_id_type=MESH,
         ).start()
-        return 0
-
-    lax.fori_loop(1, N_SPACE, send_part, 0)
     for c in images:
         c.wait()
     pltpu.make_async_copy(others, others, sems.at[0, 6]).wait()
@@ -228,38 +253,56 @@
     pltpu.make_async_copy(rest, rest, sems.at[1, 9]).wait()
     parts[slab] = part[...]
 
+    total_ref[...] = jnp.sum(parts[...], axis=0)
+    images_ref[0] = around[0]
+    images_ref[1] = raw[0]
+    images_ref[2] = around[1]
+    pltpu.make_async_copy(rest, rest, sems.at[0, 9]).wait()
+
+
+def blend(images_ref, total_ref, whole_ref, out_ref, fraction_ref, out, fraction, sems):
+    image = lax.axis_index("image")
     lane = lax.broadcasted_iota(jnp.int32, (1, BLOCK), 1)
-    total = jnp.sum(parts[...], axis=0)
-    lengths = jnp.sqrt(total * (1.0 / SCALE**2) + EPSILON)
+    lengths = jnp.sqrt(total_ref[...] * (1.0 / SCALE**2) + EPSILON)
     lengths = jnp.where((lane > 0) & (lane < IMAGES), lengths, 0.0)
 
     def arc(k):
         return jnp.sum(jnp.where(lane <= k, lengths, 0.0), axis=1, keepdims=True)
 
-    lower = bracket[0]
     full = arc(IMAGES - 1)
+    fraction[...] = jnp.broadcast_to(arc(image) / full, (1, BLOCK))
+    lower = whole_ref[NEIGHBOURS : NEIGHBOURS + 1, :BLOCK]
+    code = whole_ref[NEIGHBOURS + 1 : NEIGHBOURS + 2, :BLOCK]
     arc_lower = arc(lower)
-    place = jnp.full((1, 1), lower, jnp.int32).astype(F32) + jnp.full((1, 1), code[0], jnp.int32).astype(F32) / CODE_SCALE
+    place = lower.astype(F32) + code.astype(F32) / CODE_SCALE
     weight = (place / (IMAGES - 1) * full - arc_lower) / (arc(lower + 1) - arc_lower)
-    fraction_ref[...] = jnp.broadcast_to(arc(image) / full, (1, BLOCK))
     earlier = lower < image
     for c in range(3):
-        here = raw[0, c]
-        below = jnp.where(earlier, around[0, c], here)
-        above = jnp.where(earlier, here, around[1, c])
-        out_ref[c] = ((1.0 - weight) * below + weight * above) * (1.0 / SCALE)
-    pltpu.make_async_copy(rest, rest, sems.at[0, 9]).wait()
+        here = images_ref[1, c]
+        below = jnp.where(earlier, images_ref[0, c], here)
+        above = jnp.where(earlier, here, images_ref[2, c])
+        out[c] = ((1.0 - weight) * below + weight * above) * (1.0 / SCALE)
+    stores = [pltpu.make_async_copy(s, d, sems.at[i]) for i, (s, d) in enumerate([(out, out_ref), (fraction, fraction_ref)])]
+    for c in stores:
+        c.start()
+    for c in stores:
+        c.wait()
 
 
 def body(positions, neighbours, brackets, codes):
-    vmem, smem = (pl.BlockSpec(memory_space=s) for s in (pltpu.VMEM, pltpu.SMEM))
+    vmem = pl.BlockSpec(memory_space=pltpu.VMEM)
     rounds = len(ROUNDS)
-    out, fraction = pl.pallas_call(
+    along = [jnp.broadcast_to(v[:, None], (1, BLOCKS)) for v in (brackets, codes)]
+    whole = jnp.concatenate([neighbours.T] + along, axis=0)
+    images, total = pl.pallas_call(
         kernel,
-        out_shape=(jax.ShapeDtypeStruct((3, NB, BLOCK), F32), jax.ShapeDtypeStruct((1, BLOCK), F32)),
-        in_specs=[vmem, smem, smem, smem],
+        out_shape=(jax.ShapeDtypeStruct((3, 3, NB, BLOCK), F32), jax.ShapeDtypeStruct((1, BLOCK), F32)),
+        in_specs=[vmem] * 2,
         out_specs=(vmem, vmem),
         scratch_shapes=[
+            pltpu.SMEM((NEIGHBOURS + 2, BLOCKS), jnp.int32),
+            pltpu.SemaphoreType.DMA,
+            pltpu.SemaphoreType.REGULAR((4,)),
             pltpu.VMEM((EXT, 8, BLOCK), F32),
             pltpu.VMEM((3, 8, BLOCK), F32),
             pltpu.VMEM((EXT, BLOCK, 48), BF16),
@@ -275,7 +318,20 @@
             pltpu.SemaphoreType.DMA((2, 10)),
         ],
         compiler_params=pltpu.CompilerParams(collective_id=0, has_side_effects=True, vmem_limit_bytes=48 << 20),
-    )(positions.reshape(3, NB, BLOCK), neighbours.T, brackets, codes)
+    )(positions.reshape(3, NB, BLOCK), whole)
+    hbm = pl.BlockSpec(memory_space=pl.ANY)
+    out, fraction = pl.pallas_call(
+        blend,
+        out_shape=(jax.ShapeDtypeStruct((3, NB, BLOCK), F32), jax.ShapeDtypeStruct((1, BLOCK), F32)),
+        in_specs=[vmem] * 3,
+        out_specs=(hbm, hbm),
+        scratch_shapes=[
+            pltpu.VMEM((3, NB, BLOCK), F32),
+            pltpu.VMEM((1, BLOCK), F32),
+            pltpu.SemaphoreType.DMA((2,)),
+        ],
+        compiler_params=pltpu.CompilerParams(vmem_limit_bytes=16 << 20),
+    )(images, total, whole)
     return out.reshape(1, 3, NB * BLOCK), fraction[0, :1]
 
 

time: 54.2 us -> 48.4 us (0.89)
  Pallas kernels: 49.5 us -> 46.1 us
  between operations: 3.13 us -> 1.96 us
  local copies, waits for them, and re-layouts: 1.31 us -> 0.16 us
    pallas_call x1 -> x2, Pallas kernels: 49.5 us -> 46.1 us  [the longest x1 45.3 us: body(): pl.pallas_call(kernel, out_shape=(jax.ShapeDtypeStruct((3, 3, NB, BLOCK),...]
    unnamed x5 -> x4, local copies, waits for them, and re-layouts: 1.31 us -> 0.01 us
where the time goes in v2:
time: 48.4 us; the launch traced here: 48.3 us
  Pallas kernels  46.1 us (95%)
  between operations  1.96 us (4%)
    pallas_call x1, Pallas kernels, body(): pl.pallas_call(kernel, out_shape=(jax.ShapeDtypeStruct((3, 3, NB, BLOCK),...  45.3 us

profile of v2, /device:TPU:1, one launch (start us, length us, event | category | flops | bytes accessed | tf_op | source)
XLA Modules:
  0.0 48.3 jit_solution(6250621825455352879)
XLA Ops:
  0.6 0.0 copy-start.1
  0.6 0.0 copy-start
  2.0 0.1 pad.1.clone
  2.0 0.1 pad.2.clone
  2.1 0.0 copy-done.1
  2.1 0.1 add_add_fusion.table_in.whole_ref
  2.2 0.0 copy-done
  2.2 45.3 %shard_map.59 = (f32[3,3,8,128]{3,2,1,0:T(8,128)S(1)}, f32[1,128]{1,0:T(1,128)S(1)}) custom-call(f32[3,8,128]{2,1,0:T(8,128)S(1)} %bitcast.7, s32[5,256]{1,0:T(8,128)S(1)} %add_add_fusion.table_in.whole_ref), custom_call_target="tpu_custom_call" | custom-call | tf_op jit(solution)/shard_map/pallas_call | solution.py:297
  47.5 0.7 %shard_map.60 = (f32[3,8,128]{2,1,0:T(8,128)}, f32[1,128]{1,0:T(1,128)}) custom-call(f32[3,3,8,128]{3,2,1,0:T(8,128)S(1)} %get-tuple-element.6.images_ref, f32[1,128]{1,0:T(1,128)S(1)} %get-tuple-element.7.total_ref, s32[5,256]{1,0:T(8,128)S(1)} %add_add_fusion.table_in.whole_ref), custom_call_target="tpu_custom_call" | custom-call | tf_op jit(solution)/shard_map/pallas_call | solution.py:323
Async XLA Ops:
  0.6 1.5 %copy-start.1 = (s32[256,3]{0,1:T(4,128)S(1)}, s32[256,3]{0,1:T(4,128)}, u32[]{:S(2)}) copy-start(s32[256,3]{0,1:T(4,128)} %param.5) | copy-start | bytes 9220
  0.6 1.5 %copy-start = (f32[1,3,1024]{2,0,1:T(1,128)S(1)}, f32[1,3,1024]{2,0,1:T(1,128)}, u32[]{:S(2)}) copy-start(f32[1,3,1024]{2,0,1:T(1,128)} %param.4) | copy-start | bytes 36868

commit v3 on v2

--- a/solution.py
+++ b/solution.py
@@ -25,13 +25,12 @@
 EPSILON = 1e-06
 CODE_SCALE = 65536.0
 
-ROUNDS = (4, 3, 3)
-OWN = NB
-EXT = 3 * NB
+FIRST, LAST = 4, 6
+OWN = 2 * NB
+EXT = 5 * NB
 
 SCALE = math.sqrt(KERNEL_RATE * math.log2(math.e))
 PULL = TIME_STEP * COUPLING / (NEIGHBOURS * BLOCK)
-PARTS = 32
 
 
 def dot(a, b):
@@ -104,47 +103,27 @@
     load = pltpu.make_async_copy(table_in, table, local_sem)
     load.start()
 
-    def store_operands(lo, y):
+    def store(version, lo, y):
         a, b, x = operands(y)
         n = y.shape[0]
-        bop[lo : lo + n] = b
-        xop[lo : lo + n] = x
+        cur[version, lo : lo + n] = y
+        bop[version, lo : lo + n] = b
+        xop[version, lo : lo + n] = x
         for i in range(n):
-            aop[lo + i] = a[i].T.astype(BF16)
-
-    def take_slab(lo, slab_ref, scale):
-        pad = jnp.zeros((NB, 5, BLOCK), F32)
-        rows = [slab_ref[c].reshape(NB, 1, BLOCK) for c in range(3)]
-        y = jnp.concatenate(rows + [pad], axis=1) * scale
-        cur[lo : lo + NB] = y
-        store_operands(lo, y)
-        return y
-
-    def exchange(r, source):
-        copies = []
-        for side, d in enumerate((1, -1)):
-            copies.append(
-                pltpu.make_async_remote_copy(
-                    src_ref=source,
-                    dst_ref=got.at[r, side],
-                    send_sem=sems.at[0, 2 * r + side],
-                    recv_sem=sems.at[1, 2 * r + side],
-                    device_id=beside(d),
-                    device_id_type=MESH,
-                )
-            )
-        return copies
-
-    pl.semaphore_wait(barrier, len(near))
-    copies = exchange(0, x_ref)
-    for c in copies:
-        c.start()
-    relay(0)
-    own = take_slab(OWN, x_ref, SCALE)
-    anchor[1] = own[0]
-    load.wait()
-
-    def step(lo, n):
+            aop[version, lo + i] = a[i].T.astype(BF16)
+
+    def rows(slab_ref, first, last):
+        n = last - first
+        coordinates = [slab_ref[c, first:last].reshape(n, 1, BLOCK) for c in range(3)]
+        return jnp.concatenate(coordinates + [jnp.zeros((n, 5, BLOCK), F32)], axis=1)
+
+    def send(source, target, slot, peer):
+        return pltpu.make_async_remote_copy(
+            src_ref=source, dst_ref=target, send_sem=sems.at[0, slot], recv_sem=sems.at[1, slot],
+            device_id=peer, device_id_type=MESH,
+        )
+
+    def step(version, lo, n):
         blocks = range(lo, lo + n)
         first = slab * NB + BLOCKS - OWN
         partners = [
@@ -153,16 +132,16 @@
         ]
         weights = []
         for e, ps in zip(blocks, partners):
-            exponent = dot(jnp.concatenate([aop[p] for p in ps], axis=0), bop[e])
+            exponent = dot(jnp.concatenate([aop[version, p] for p in ps], axis=0), bop[version, e])
             w = jnp.exp2(exponent)
             high = w.astype(BF16)
             weights.append(jnp.concatenate([high, (w - high.astype(F32)).astype(BF16)], axis=0))
         sums = []
         for ps, w in zip(partners, weights):
-            x = jnp.concatenate([xop[p] for p in ps], axis=1)
+            x = jnp.concatenate([xop[version, p] for p in ps], axis=1)
             total = dot(jnp.concatenate([x, x], axis=1), w)
             sums.append(total[0:8] + total[8:16] + total[16:24])
-        y = cur[lo : lo + n]
+        y = cur[version, lo : lo + n]
         total = jnp.stack(sums, axis=0)
         y_new = y + PULL * (y * total[:, 4:5] - total)
         held = [
@@ -171,66 +150,82 @@
             else y_new[i : i + 1]
             for i, e in enumerate(blocks)
         ]
-        y_new = jnp.concatenate(held, axis=0)
-        cur[lo : lo + n] = y_new
-        return y_new
-
-    def steps(count, last, between):
-        for t in range(count - last):
-            reach = HALO * (count - 1 - t)
-            lo, n = OWN - reach, NB + 2 * reach
-            y = step(lo, n)
-            if t < count - 1:
-                store_operands(lo, y)
-            if t in between:
-                relay(between[t])
-        return y
+        return jnp.concatenate(held, axis=0) if n > 1 else held[0]
 
     def pack(ref, y):
         for c in range(3):
             ref[c] = y[:, c]
 
-    for c in copies:
+    pl.semaphore_wait(barrier, len(near))
+    from_left, from_right, from_right2 = (got.at[i] for i in range(3))
+    beginning = [send(x_ref, from_left, 0, beside(1)), send(x_ref, from_right, 1, beside(-1))]
+    for c in beginning:
+        c.start()
+    relay(0)
+    own = rows(x_ref, 0, NB) * SCALE
+    anchor[2] = own[0]
+    store(0, OWN, own)
+    load.wait()
+    for c in beginning:
         c.wait()
     relay(1)
-    anchor[0] = take_slab(0, got.at[0, 0], SCALE)[0]
-    anchor[2] = take_slab(2 * NB, got.at[0, 1], SCALE)[0]
-    y = steps(ROUNDS[0], 0, {1: 2})
-    for r in range(1, len(ROUNDS)):
-        pack(raw.at[r], y)
-        copies = exchange(r, raw.at[r])
-        for c in copies:
-            c.start()
-        store_operands(OWN, y)
-        for c in copies:
-            c.wait()
-        take_slab(0, got.at[r, 0], 1.0)
-        take_slab(2 * NB, got.at[r, 1], 1.0)
-        if r == 1:
-            relay(3)
-        y = steps(ROUNDS[r], int(r == len(ROUNDS) - 1), {})
+    later = send(x_ref, from_right2, 2, beside(-2))
+    later.start()
+    left = rows(from_left, 0, NB) * SCALE
+    right = rows(from_right, 0, NB) * SCALE
+    anchor[1] = left[0]
+    anchor[3] = right[0]
+    store(0, OWN - NB, left)
+    store(0, OWN + NB, right)
+    for t in range(FIRST):
+        reach = HALO * (FIRST - 1 - t)
+        y = step(0, OWN - reach, NB + 2 * reach)
+        if t < FIRST - 1:
+            store(0, OWN - reach, y)
+        if t == 1:
+            relay(2)
+
+    pack(raw.at[1], y)
+    middle = [send(raw.at[1], got.at[3 + i], 3 + i, beside(d)) for i, d in enumerate((2, -2, 1, -1))]
+    for c in middle:
+        c.start()
+    store(0, OWN, y)
+    for c in middle:
+        c.wait()
+    relay(3)
+    left2, right2, left, right = (got.at[3 + i] for i in range(4))
+    reach = HALO * LAST - NB
+    store(0, OWN - NB - reach, jnp.concatenate([rows(left2, NB - reach, NB), rows(left, 0, NB)], axis=0))
+    store(0, OWN + NB, rows(right, 0, reach + 1))
+
+    for s in range(1, LAST + 1):
+        reach = HALO * (LAST - s)
+        head = step(s - 1, OWN - reach, 2 * reach + 1)
+        if s < LAST:
+            store(s, OWN - reach, head)
     relay(4)
 
     row = lax.broadcasted_iota(jnp.int32, (8, BLOCK), 0)
-    head = step(OWN, 1)
     mine[...] = jnp.where(row < 3, head[0], 0.0)[0:4]
     for d in square:
-        pltpu.make_async_remote_copy(
-            src_ref=mine, dst_ref=plane.at[image], send_sem=sems.at[0, 6], recv_sem=sems.at[1, 6],
-            device_id=in_plane(d), device_id_type=MESH,
-        ).start()
-    pack(raw.at[0], jnp.concatenate([head, step(OWN + 1, NB - 1)], axis=0))
-    images = [
-        pltpu.make_async_remote_copy(
-            src_ref=raw.at[0], dst_ref=around.at[side], send_sem=sems.at[0, 7 + side], recv_sem=sems.at[1, 7 + side],
-            device_id=across(d), device_id_type=MESH,
-        )
-        for side, d in enumerate((1, -1))
-    ]
-    for c in images:
-        c.start()
+        send(mine, plane.at[image], 7, in_plane(d)).start()
+
+    later.wait()
+    anchor[4] = rows(from_right2, 0, 1)[0] * SCALE
+    reach = HALO * LAST - NB
+    store(0, OWN + NB + reach + 1, jnp.concatenate([rows(right, reach + 1, NB), rows(right2, 0, reach)], axis=0))
+
+    def rest_of_step(s):
+        lo = OWN + HALO * (LAST - s) + 1
+        y = step(s - 1, lo, NB - 1)
+        if s < LAST:
+            store(s, lo, y)
+        return y
+
+    for s in range(1, LAST):
+        rest_of_step(s)
     others = plane.at[pl.ds(1, IMAGES - 1)]
-    pltpu.make_async_copy(others, others, sems.at[1, 6]).wait()
+    pltpu.make_async_copy(others, others, sems.at[1, 7]).wait()
     plane[image] = mine[...]
 
     every = plane[...]
@@ -242,22 +237,23 @@
     part[...] = jnp.sum(jnp.where(at_row == at_lane, squares, 0.0), axis=0, keepdims=True)
 
     for d in ring:
-        pltpu.make_async_remote_copy(
-            src_ref=part, dst_ref=parts.at[slab], send_sem=sems.at[0, 9], recv_sem=sems.at[1, 9],
-            device_id=beside(d), device_id_type=MESH,
-        ).start()
+        send(part, parts.at[slab], 10, beside(d)).start()
+    pack(raw.at[0], jnp.concatenate([head, rest_of_step(LAST)], axis=0))
+    images = [send(raw.at[0], around.at[i], 8 + i, across(d)) for i, d in enumerate((1, -1))]
+    for c in images:
+        c.start()
     for c in images:
         c.wait()
-    pltpu.make_async_copy(others, others, sems.at[0, 6]).wait()
+    pltpu.make_async_copy(others, others, sems.at[0, 7]).wait()
     rest = parts.at[pl.ds(1, N_SPACE - 1)]
-    pltpu.make_async_copy(rest, rest, sems.at[1, 9]).wait()
+    pltpu.make_async_copy(rest, rest, sems.at[1, 10]).wait()
     parts[slab] = part[...]
 
     total_ref[...] = jnp.sum(parts[...], axis=0)
     images_ref[0] = around[0]
     images_ref[1] = raw[0]
     images_ref[2] = around[1]
-    pltpu.make_async_copy(rest, rest, sems.at[0, 9]).wait()
+    pltpu.make_async_copy(rest, rest, sems.at[0, 10]).wait()
 
 
 def blend(images_ref, total_ref, whole_ref, out_ref, fraction_ref, out, fraction, sems):
@@ -291,7 +287,6 @@
 
 def body(positions, neighbours, brackets, codes):
     vmem = pl.BlockSpec(memory_space=pltpu.VMEM)
-    rounds = len(ROUNDS)
     along = [jnp.broadcast_to(v[:, None], (1, BLOCKS)) for v in (brackets, codes)]
     whole = jnp.concatenate([neighbours.T] + along, axis=0)
     images, total = pl.pallas_call(
@@ -303,19 +298,19 @@
             pltpu.SMEM((NEIGHBOURS + 2, BLOCKS), jnp.int32),
             pltpu.SemaphoreType.DMA,
             pltpu.SemaphoreType.REGULAR((4,)),
-            pltpu.VMEM((EXT, 8, BLOCK), F32),
-            pltpu.VMEM((3, 8, BLOCK), F32),
-            pltpu.VMEM((EXT, BLOCK, 48), BF16),
-            pltpu.VMEM((EXT, 48, BLOCK), BF16),
-            pltpu.VMEM((EXT, 32, BLOCK), BF16),
-            pltpu.VMEM((rounds, 3, NB, BLOCK), F32),
-            pltpu.VMEM((rounds, 2, 3, NB, BLOCK), F32),
+            pltpu.VMEM((LAST, EXT, 8, BLOCK), F32),
+            pltpu.VMEM((EXT // NB, 8, BLOCK), F32),
+            pltpu.VMEM((LAST, EXT, BLOCK, 48), BF16),
+            pltpu.VMEM((LAST, EXT, 48, BLOCK), BF16),
+            pltpu.VMEM((LAST, EXT, 32, BLOCK), BF16),
+            pltpu.VMEM((2, 3, NB, BLOCK), F32),
+            pltpu.VMEM((7, 3, NB, BLOCK), F32),
             pltpu.VMEM((2, 3, NB, BLOCK), F32),
             pltpu.VMEM((IMAGES, 4, BLOCK), F32),
             pltpu.VMEM((4, BLOCK), F32),
             pltpu.VMEM((1, BLOCK), F32),
             pltpu.VMEM((N_SPACE, 1, BLOCK), F32),
-            pltpu.SemaphoreType.DMA((2, 10)),
+            pltpu.SemaphoreType.DMA((2, 11)),
         ],
         compiler_params=pltpu.CompilerParams(collective_id=0, has_side_effects=True, vmem_limit_bytes=48 << 20),
     )(positions.reshape(3, NB, BLOCK), whole)

time: 48.4 us -> 45.6 us (0.942)
  Pallas kernels: 46.1 us -> 43.3 us
    pallas_call x1, Pallas kernels: 45.3 us -> 42.6 us  [body(): pl.pallas_call(kernel, out_shape=(jax.ShapeDtypeStruct((3, 3, NB, BLOCK),...]
where the time goes in v3:
time: 45.6 us; the launch traced here: 45.5 us
  Pallas kernels  43.3 us (95%)
  between operations  1.96 us (4%)
    pallas_call x1, Pallas kernels, body(): pl.pallas_call(kernel, out_shape=(jax.ShapeDtypeStruct((3, 3, NB, BLOCK),...  42.6 us

profile of v3, /device:TPU:1, one launch (start us, length us, event | category | flops | bytes accessed | tf_op | source)
XLA Modules:
  0.0 45.5 jit_solution(9357721979916494421)
XLA Ops:
  0.6 0.0 copy-start.1
  0.6 0.0 copy-start
  2.0 0.1 pad.1.clone
  2.0 0.1 pad.2.clone
  2.1 0.0 copy-done.1
  2.1 0.1 add_add_fusion.table_in.whole_ref
  2.2 0.0 copy-done
  2.2 42.6 %shard_map.59 = (f32[3,3,8,128]{3,2,1,0:T(8,128)S(1)}, f32[1,128]{1,0:T(1,128)S(1)}) custom-call(f32[3,8,128]{2,1,0:T(8,128)S(1)} %bitcast.7, s32[5,256]{1,0:T(8,128)S(1)} %add_add_fusion.table_in.whole_ref), custom_call_target="tpu_custom_call" | custom-call | tf_op jit(solution)/shard_map/pallas_call | solution.py:292
  44.7 0.7 %shard_map.60 = (f32[3,8,128]{2,1,0:T(8,128)}, f32[1,128]{1,0:T(1,128)}) custom-call(f32[3,3,8,128]{3,2,1,0:T(8,128)S(1)} %get-tuple-element.6.images_ref, f32[1,128]{1,0:T(1,128)S(1)} %get-tuple-element.7.total_ref, s32[5,256]{1,0:T(8,128)S(1)} %add_add_fusion.table_in.whole_ref), custom_call_target="tpu_custom_call" | custom-call | tf_op jit(solution)/shard_map/pallas_call | solution.py:318
Async XLA Ops:
  0.6 1.5 %copy-start.1 = (s32[256,3]{0,1:T(4,128)S(1)}, s32[256,3]{0,1:T(4,128)}, u32[]{:S(2)}) copy-start(s32[256,3]{0,1:T(4,128)} %param.5) | copy-start | bytes 9220
  0.6 1.5 %copy-start = (f32[1,3,1024]{2,0,1:T(1,128)S(1)}, f32[1,3,1024]{2,0,1:T(1,128)}, u32[]{:S(2)}) copy-start(f32[1,3,1024]{2,0,1:T(1,128)} %param.4) | copy-start | bytes 36868

commit v4 on v3

--- a/solution.py
+++ b/solution.py
@@ -59,7 +59,7 @@
 
 
 def kernel(
-    x_ref, table_in, images_ref, total_ref,
+    x_ref, left_ref, right_ref, table_in, images_ref, total_ref,
     table, local_sem, relay_sems, cur, anchor, aop, bop, xop, raw, got, around, plane, mine, part, parts, sems,
 ):
     image, slab = lax.axis_index("image"), lax.axis_index("space")
@@ -82,15 +82,11 @@
             pl.semaphore_signal(semaphore, inc=1, device_id=peer, device_id_type=MESH)
 
     barrier = pltpu.get_barrier_semaphore()
-    near = [beside(1), beside(-1), across(1), across(-1)]
+    near = [peer for d in (1, -1, 2, -2) for peer in (beside(d), across(d))]
     stages = [
-        [peer for far in reach for peer in far]
-        for reach in (
-            [(beside(1), beside(-1)), (across(1), across(-1))],
-            [(beside(2), beside(-2)), (across(2), across(-2))],
-            [(beside(4), beside(-4)), (across(4), across(-4))],
-            [(beside(8), beside(-8))],
-        )
+        [peer for d in (2, -2) for peer in (beside(d), across(d))],
+        [peer for d in (4, -4) for peer in (beside(d), across(d))],
+        [beside(8), beside(-8)],
     ]
 
     def relay(j):
@@ -156,44 +152,31 @@
         for c in range(3):
             ref[c] = y[:, c]
 
-    pl.semaphore_wait(barrier, len(near))
-    from_left, from_right, from_right2 = (got.at[i] for i in range(3))
-    beginning = [send(x_ref, from_left, 0, beside(1)), send(x_ref, from_right, 1, beside(-1))]
-    for c in beginning:
-        c.start()
-    relay(0)
-    own = rows(x_ref, 0, NB) * SCALE
-    anchor[2] = own[0]
-    store(0, OWN, own)
+    own, left, right = (rows(ref, 0, NB) * SCALE for ref in (x_ref, left_ref, right_ref))
+    for i, y in enumerate((left, own, right)):
+        anchor[1 + i] = y[0]
+        store(0, OWN + (i - 1) * NB, y)
     load.wait()
-    for c in beginning:
-        c.wait()
-    relay(1)
-    later = send(x_ref, from_right2, 2, beside(-2))
-    later.start()
-    left = rows(from_left, 0, NB) * SCALE
-    right = rows(from_right, 0, NB) * SCALE
-    anchor[1] = left[0]
-    anchor[3] = right[0]
-    store(0, OWN - NB, left)
-    store(0, OWN + NB, right)
     for t in range(FIRST):
         reach = HALO * (FIRST - 1 - t)
         y = step(0, OWN - reach, NB + 2 * reach)
         if t < FIRST - 1:
             store(0, OWN - reach, y)
         if t == 1:
-            relay(2)
+            pl.semaphore_wait(barrier, len(near))
+            relay(0)
+            later = send(x_ref, got.at[0], 0, beside(-2))
+            later.start()
 
     pack(raw.at[1], y)
-    middle = [send(raw.at[1], got.at[3 + i], 3 + i, beside(d)) for i, d in enumerate((2, -2, 1, -1))]
+    middle = [send(raw.at[1], got.at[1 + i], 1 + i, beside(d)) for i, d in enumerate((2, -2, 1, -1))]
     for c in middle:
         c.start()
     store(0, OWN, y)
     for c in middle:
         c.wait()
-    relay(3)
-    left2, right2, left, right = (got.at[3 + i] for i in range(4))
+    relay(1)
+    left2, right2, left, right = (got.at[1 + i] for i in range(4))
     reach = HALO * LAST - NB
     store(0, OWN - NB - reach, jnp.concatenate([rows(left2, NB - reach, NB), rows(left, 0, NB)], axis=0))
     store(0, OWN + NB, rows(right, 0, reach + 1))
@@ -203,7 +186,7 @@
         head = step(s - 1, OWN - reach, 2 * reach + 1)
         if s < LAST:
             store(s, OWN - reach, head)
-    relay(4)
+    relay(2)
 
     row = lax.broadcasted_iota(jnp.int32, (8, BLOCK), 0)
     mine[...] = jnp.where(row < 3, head[0], 0.0)[0:4]
@@ -211,7 +194,7 @@
         send(mine, plane.at[image], 7, in_plane(d)).start()
 
     later.wait()
-    anchor[4] = rows(from_right2, 0, 1)[0] * SCALE
+    anchor[4] = rows(got.at[0], 0, 1)[0] * SCALE
     reach = HALO * LAST - NB
     store(0, OWN + NB + reach + 1, jnp.concatenate([rows(right, reach + 1, NB), rows(right2, 0, reach)], axis=0))
 
@@ -236,6 +219,7 @@
     at_lane = lax.broadcasted_iota(jnp.int32, (IMAGES, BLOCK), 1)
     part[...] = jnp.sum(jnp.where(at_row == at_lane, squares, 0.0), axis=0, keepdims=True)
 
+    relay(3)
     for d in ring:
         send(part, parts.at[slab], 10, beside(d)).start()
     pack(raw.at[0], jnp.concatenate([head, rest_of_step(LAST)], axis=0))
@@ -287,24 +271,27 @@
 
 def body(positions, neighbours, brackets, codes):
     vmem = pl.BlockSpec(memory_space=pltpu.VMEM)
+    left, right = (
+        lax.ppermute(positions, "space", [(i, (i + d) % N_SPACE) for i in range(N_SPACE)]) for d in (1, -1)
+    )
     along = [jnp.broadcast_to(v[:, None], (1, BLOCKS)) for v in (brackets, codes)]
     whole = jnp.concatenate([neighbours.T] + along, axis=0)
     images, total = pl.pallas_call(
         kernel,
         out_shape=(jax.ShapeDtypeStruct((3, 3, NB, BLOCK), F32), jax.ShapeDtypeStruct((1, BLOCK), F32)),
-        in_specs=[vmem] * 2,
+        in_specs=[vmem] * 4,
         out_specs=(vmem, vmem),
         scratch_shapes=[
             pltpu.SMEM((NEIGHBOURS + 2, BLOCKS), jnp.int32),
             pltpu.SemaphoreType.DMA,
-            pltpu.SemaphoreType.REGULAR((4,)),
+            pltpu.SemaphoreType.REGULAR((3,)),
             pltpu.VMEM((LAST, EXT, 8, BLOCK), F32),
             pltpu.VMEM((EXT // NB, 8, BLOCK), F32),
             pltpu.VMEM((LAST, EXT, BLOCK, 48), BF16),
             pltpu.VMEM((LAST, EXT, 48, BLOCK), BF16),
             pltpu.VMEM((LAST, EXT, 32, BLOCK), BF16),
             pltpu.VMEM((2, 3, NB, BLOCK), F32),
-            pltpu.VMEM((7, 3, NB, BLOCK), F32),
+            pltpu.VMEM((5, 3, NB, BLOCK), F32),
             pltpu.VMEM((2, 3, NB, BLOCK), F32),
             pltpu.VMEM((IMAGES, 4, BLOCK), F32),
             pltpu.VMEM((4, BLOCK), F32),
@@ -313,7 +300,7 @@
             pltpu.SemaphoreType.DMA((2, 11)),
         ],
         compiler_params=pltpu.CompilerParams(collective_id=0, has_side_effects=True, vmem_limit_bytes=48 << 20),
-    )(positions.reshape(3, NB, BLOCK), whole)
+    )(*(x.reshape(3, NB, BLOCK) for x in (positions, left, right)), whole)
     hbm = pl.BlockSpec(memory_space=pl.ANY)
     out, fraction = pl.pallas_call(
         blend,

time: 45.6 us -> 44.3 us (0.971)
  Pallas kernels: 43.3 us -> 32.2 us
  starting transfers between devices: 0 us -> 6.89 us
  waiting for transfers between devices: 0 us -> 2.88 us
    pallas_call x1, Pallas kernels: 42.6 us -> 31.4 us  [body(): pl.pallas_call(kernel, out_shape=(jax.ShapeDtypeStruct((3, 3, NB, BLOCK),...]
    ppermute x0 -> x2, starting transfers between devices: none -> 6.89 us  [body(): lax.ppermute(positions, 'space', [(i, (i + d) % N_SPACE) for i in range(N...]
    ppermute x0 -> x2, waiting for transfers between devices: none -> 2.88 us  [body(): lax.ppermute(positions, 'space', [(i, (i + d) % N_SPACE) for i in range(N...]
  transfers between devices with their start and end apart: 0 -> 2, of which waited for: 0 -> 1; matrix products, arithmetic and copies ran while one was open for 0% -> 0% of each run, Pallas kernels for 0% -> 0%
where the time goes in v4:
time: 44.3 us; the launch traced here: 44.1 us
  Pallas kernels  32.2 us (73%)
  starting transfers between devices  6.89 us (16%)
  waiting for transfers between devices  2.88 us (7%)
  between operations  1.97 us (4%)
    pallas_call x1, Pallas kernels, body(): pl.pallas_call(kernel, out_shape=(jax.ShapeDtypeStruct((3, 3, NB, BLOCK),...  31.4 us
    ppermute x2, starting transfers between devices, body(): lax.ppermute(positions, 'space', [(i, (i + d) % N_SPACE) for i in range(N...  6.89 us
    ppermute x2, waiting for transfers between devices, body(): lax.ppermute(positions, 'space', [(i, (i + d) % N_SPACE) for i in range(N...  2.88 us
  transfers between devices with their start and end apart: 2, of which 1 were waited for; matrix products, arithmetic and copies ran while one was open for 0% of the time, Pallas kernels for 0%

profile of v4, /device:TPU:1, one launch (start us, length us, event | category | flops | bytes accessed | tf_op | source)
XLA Modules:
  0.0 44.1 jit_solution(12644023512495580596)
XLA Ops:
  0.6 6.9 %collective-permute-start.1 = (f32[1,3,1024]{2,0,1:T(1,128)}, f32[1,3,1024]{2,0,1:T(1,128)S(1)}, u32[]{:S(2)}, u32[]{:S(2)}) collective-permute-start(f32[1,3,1024]{2,0,1:T(1,128)} %param.4), channel_id=1, source_target_pairs={{0,31},{1,0},{2,1},{3,2},{4,3},{5,4},{6,5},{7,6},{8,7},{9,8},{10,9... | collective-permute-start | bytes 36872 | tf_op jit(solution)/shard_map/ppermute | solution.py:275
  7.5 0.0 collective-permute-start
  8.2 0.0 copy-start.1
  8.8 0.0 copy-start
  8.9 0.1 pad.1.clone
  8.9 0.1 pad.2.clone
  9.0 0.0 copy-done.1
  9.0 0.1 add_add_fusion.table_in.whole_ref
  9.1 0.0 collective-permute-done.1
  9.1 2.9 %collective-permute-done = f32[1,3,1024]{2,0,1:T(1,128)S(1)} collective-permute-done((f32[1,3,1024]{2,0,1:T(1,128)}, f32[1,3,1024]{2,0,1:T(1,128)S(1)}, u32[]{:S(2)}, u32[]{:S(2)}) %collective-permute-start) | collective-permute-done | bytes 12320 | tf_op jit(solution)/shard_map/ppermute | solution.py:275
  12.0 0.0 copy-done
  12.0 31.4 %shard_map.59 = (f32[3,3,8,128]{3,2,1,0:T(8,128)S(1)}, f32[1,128]{1,0:T(1,128)S(1)}) custom-call(f32[3,8,128]{2,1,0:T(8,128)S(1)} %bitcast.9, f32[3,8,128]{2,1,0:T(8,128)S(1)} %bitcast.11, f32[3,8,128]{2,1,0:T(8,128)S(1)} %bitcast.10, s32[5,256]{1,0:T(8,128)S(1)} %add_add_fusion.table_in.whole_ref), custom_call_target="tpu_custom_call" | custom-call | tf_op jit(solution)/shard_map/pallas_call | solution.py:279
  43.4 0.7 %shard_map.60 = (f32[3,8,128]{2,1,0:T(8,128)}, f32[1,128]{1,0:T(1,128)}) custom-call(f32[3,3,8,128]{3,2,1,0:T(8,128)S(1)} %get-tuple-element.6.images_ref, f32[1,128]{1,0:T(1,128)S(1)} %get-tuple-element.7.total_ref, s32[5,256]{1,0:T(8,128)S(1)} %add_add_fusion.table_in.whole_ref), custom_call_target="tpu_custom_call" | custom-call | tf_op jit(solution)/shard_map/pallas_call | solution.py:305
Async XLA Ops:
  0.6 8.5 %collective-permute-start.1 = (f32[1,3,1024]{2,0,1:T(1,128)}, f32[1,3,1024]{2,0,1:T(1,128)S(1)}, u32[]{:S(2)}, u32[]{:S(2)}) collective-permute-start(f32[1,3,1024]{2,0,1:T(1,128)} %param.4), channel_id=1, source_target_pairs={{0,31},{1,0},{2,1},{3,2},{4,3},{5,4},{6,5},{7,6},{8,7},{9,8},{10,9... | collective-permute-start | bytes 36872 | tf_op jit(solution)/shard_map/ppermute | solution.py:275
  7.5 4.4 %collective-permute-start = (f32[1,3,1024]{2,0,1:T(1,128)}, f32[1,3,1024]{2,0,1:T(1,128)S(1)}, u32[]{:S(2)}, u32[]{:S(2)}) collective-permute-start(f32[1,3,1024]{2,0,1:T(1,128)} %param.4), channel_id=1, source_target_pairs={{0,1},{1,2},{2,3},{3,4},{4,5},{5,6},{6,7},{7,8},{8,9},{9,10},{10,1... | collective-permute-start | bytes 36872 | tf_op jit(solution)/shard_map/ppermute | solution.py:275
  8.2 0.8 %copy-start.1 = (s32[256,3]{0,1:T(4,128)S(1)}, s32[256,3]{0,1:T(4,128)}, u32[]{:S(2)}) copy-start(s32[256,3]{0,1:T(4,128)} %param.5) | copy-start | bytes 9220
  8.8 3.1 %copy-start = (f32[1,3,1024]{2,0,1:T(1,128)S(1)}, f32[1,3,1024]{2,0,1:T(1,128)}, u32[]{:S(2)}) copy-start(f32[1,3,1024]{2,0,1:T(1,128)} %param.4) | copy-start | bytes 36868

commit v5 on v4

--- a/solution.py
+++ b/solution.py
@@ -60,7 +60,7 @@
 
 def kernel(
     x_ref, left_ref, right_ref, table_in, images_ref, total_ref,
-    table, local_sem, relay_sems, cur, anchor, aop, bop, xop, raw, got, around, plane, mine, part, parts, sems,
+    table, local_sem, relay_sems, cur, anchor, aop, bop, xop, raw, ahead, halves, far, whole, around, plane, mine, part, parts, sems,
 ):
     image, slab = lax.axis_index("image"), lax.axis_index("space")
 
@@ -119,8 +119,8 @@
             device_id=peer, device_id_type=MESH,
         )
 
-    def step(version, lo, n):
-        blocks = range(lo, lo + n)
+    def step(version, *runs):
+        blocks = [e for lo, n in runs for e in range(lo, lo + n)]
         first = slab * NB + BLOCKS - OWN
         partners = [
             [e - HALO + table[k, lax.rem(first + e, BLOCKS)] for k in range(NEIGHBOURS)]
@@ -137,7 +137,8 @@
             x = jnp.concatenate([xop[version, p] for p in ps], axis=1)
             total = dot(jnp.concatenate([x, x], axis=1), w)
             sums.append(total[0:8] + total[8:16] + total[16:24])
-        y = cur[version, lo : lo + n]
+        held = [cur[version, lo : lo + n] for lo, n in runs]
+        y = jnp.concatenate(held, axis=0) if len(runs) > 1 else held[0]
         total = jnp.stack(sums, axis=0)
         y_new = y + PULL * (y * total[:, 4:5] - total)
         held = [
@@ -146,7 +147,7 @@
             else y_new[i : i + 1]
             for i, e in enumerate(blocks)
         ]
-        return jnp.concatenate(held, axis=0) if n > 1 else held[0]
+        return jnp.concatenate(held, axis=0) if len(held) > 1 else held[0]
 
     def pack(ref, y):
         for c in range(3):
@@ -159,34 +160,52 @@
     load.wait()
     for t in range(FIRST):
         reach = HALO * (FIRST - 1 - t)
-        y = step(0, OWN - reach, NB + 2 * reach)
+        y = step(0, (OWN - reach, NB + 2 * reach))
         if t < FIRST - 1:
             store(0, OWN - reach, y)
         if t == 1:
             pl.semaphore_wait(barrier, len(near))
             relay(0)
-            later = send(x_ref, got.at[0], 0, beside(-2))
+            later = send(x_ref, ahead, 0, beside(-2))
             later.start()
 
-    pack(raw.at[1], y)
-    middle = [send(raw.at[1], got.at[1 + i], 1 + i, beside(d)) for i, d in enumerate((2, -2, 1, -1))]
+    for h in range(2):
+        pack(halves.at[h], y[h * NB // 2 : (h + 1) * NB // 2])
+    left2, left, right, right2 = far.at[0], whole.at[0], whole.at[1], far.at[1]
+    middle = [
+        send(halves.at[1], left2, 1, beside(2)),
+        send(halves, left, 2, beside(1)),
+        send(halves, right, 3, beside(-1)),
+    ]
     for c in middle:
         c.start()
+    last = send(halves.at[0], right2, 4, beside(-2))
+    last.start()
     store(0, OWN, y)
+    inner = (OWN + HALO, NB - 2 * HALO)
+    store(1, inner[0], step(0, inner))
     for c in middle:
         c.wait()
     relay(1)
-    left2, right2, left, right = (got.at[1 + i] for i in range(4))
-    reach = HALO * LAST - NB
-    store(0, OWN - NB - reach, jnp.concatenate([rows(left2, NB - reach, NB), rows(left, 0, NB)], axis=0))
-    store(0, OWN + NB, rows(right, 0, reach + 1))
+    left = jnp.concatenate([rows(left2, 0, NB // 2)] + [rows(left.at[h], 0, NB // 2) for h in range(2)], axis=0)
+    store(0, OWN - NB - NB // 2, left)
+    store(0, OWN + NB, jnp.concatenate([rows(right.at[0], 0, NB // 2), rows(right.at[1], 0, 1)], axis=0))
 
     for s in range(1, LAST + 1):
         reach = HALO * (LAST - s)
-        head = step(s - 1, OWN - reach, 2 * reach + 1)
+        lo, end = OWN - reach, OWN + reach + 1
+        if s == 1:
+            n = inner[0] - lo
+            after = inner[0] + inner[1]
+            head = step(0, (lo, n), (after, end - after))
+            store(1, lo, head[:n])
+            store(1, after, head[n:])
+            continue
+        head = step(s - 1, (lo, end - lo))
         if s < LAST:
-            store(s, OWN - reach, head)
-    relay(2)
+            store(s, lo, head)
+        if s == 4:
+            relay(2)
 
     row = lax.broadcasted_iota(jnp.int32, (8, BLOCK), 0)
     mine[...] = jnp.where(row < 3, head[0], 0.0)[0:4]
@@ -194,18 +213,18 @@
         send(mine, plane.at[image], 7, in_plane(d)).start()
 
     later.wait()
-    anchor[4] = rows(got.at[0], 0, 1)[0] * SCALE
-    reach = HALO * LAST - NB
-    store(0, OWN + NB + reach + 1, jnp.concatenate([rows(right, reach + 1, NB), rows(right2, 0, reach)], axis=0))
+    anchor[4] = rows(ahead, 0, 1)[0] * SCALE
+    last.wait()
+    store(0, OWN + NB + NB // 2 + 1, jnp.concatenate([rows(right.at[1], 1, NB // 2), rows(right2, 0, NB // 2)], axis=0))
 
     def rest_of_step(s):
         lo = OWN + HALO * (LAST - s) + 1
-        y = step(s - 1, lo, NB - 1)
+        y = step(s - 1, (lo, NB - 1))
         if s < LAST:
             store(s, lo, y)
         return y
 
-    for s in range(1, LAST):
+    for s in range(1, LAST - 1):
         rest_of_step(s)
     others = plane.at[pl.ds(1, IMAGES - 1)]
     pltpu.make_async_copy(others, others, sems.at[1, 7]).wait()
@@ -222,8 +241,9 @@
     relay(3)
     for d in ring:
         send(part, parts.at[slab], 10, beside(d)).start()
-    pack(raw.at[0], jnp.concatenate([head, rest_of_step(LAST)], axis=0))
-    images = [send(raw.at[0], around.at[i], 8 + i, across(d)) for i, d in enumerate((1, -1))]
+    rest_of_step(LAST - 1)
+    pack(raw, jnp.concatenate([head, rest_of_step(LAST)], axis=0))
+    images = [send(raw, around.at[i], 8 + i, across(d)) for i, d in enumerate((1, -1))]
     for c in images:
         c.start()
     for c in images:
@@ -235,7 +255,7 @@
 
     total_ref[...] = jnp.sum(parts[...], axis=0)
     images_ref[0] = around[0]
-    images_ref[1] = raw[0]
+    images_ref[1] = raw[...]
     images_ref[2] = around[1]
     pltpu.make_async_copy(rest, rest, sems.at[0, 10]).wait()
 
@@ -290,8 +310,11 @@
             pltpu.VMEM((LAST, EXT, BLOCK, 48), BF16),
             pltpu.VMEM((LAST, EXT, 48, BLOCK), BF16),
             pltpu.VMEM((LAST, EXT, 32, BLOCK), BF16),
-            pltpu.VMEM((2, 3, NB, BLOCK), F32),
-            pltpu.VMEM((5, 3, NB, BLOCK), F32),
+            pltpu.VMEM((3, NB, BLOCK), F32),
+            pltpu.VMEM((3, NB, BLOCK), F32),
+            pltpu.VMEM((2, 3, NB // 2, BLOCK), F32),
+            pltpu.VMEM((2, 3, NB // 2, BLOCK), F32),
+            pltpu.VMEM((2, 2, 3, NB // 2, BLOCK), F32),
             pltpu.VMEM((2, 3, NB, BLOCK), F32),
             pltpu.VMEM((IMAGES, 4, BLOCK), F32),
             pltpu.VMEM((4, BLOCK), F32),

time: 44.3 us -> 43.3 us (0.977)
  Pallas kernels: 32.2 us -> 31.1 us
    pallas_call x1, Pallas kernels: 31.4 us -> 30.4 us  [body(): pl.pallas_call(kernel, out_shape=(jax.ShapeDtypeStruct((3, 3, NB, BLOCK),...]
  transfers between devices with their start and end apart: 2 -> 2, of which waited for: 1 -> 1; matrix products, arithmetic and copies ran while one was open for 0% -> 1% of each run, Pallas kernels for 0% -> 0%
where the time goes in v5:
time: 43.3 us; the launch traced here: 43.1 us
  Pallas kernels  31.1 us (72%)
  starting transfers between devices  6.89 us (16%)
  waiting for transfers between devices  2.88 us (7%)
  between operations  1.97 us (5%)
    pallas_call x1, Pallas kernels, body(): pl.pallas_call(kernel, out_shape=(jax.ShapeDtypeStruct((3, 3, NB, BLOCK),...  30.4 us
    ppermute x2, starting transfers between devices, body(): lax.ppermute(positions, 'space', [(i, (i + d) % N_SPACE) for i in range(N...  6.89 us
    ppermute x2, waiting for transfers between devices, body(): lax.ppermute(positions, 'space', [(i, (i + d) % N_SPACE) for i in range(N...  2.88 us
  transfers between devices with their start and end apart: 2, of which 1 were waited for; matrix products, arithmetic and copies ran while one was open for 1% of the time, Pallas kernels for 0%

profile of v5, /device:TPU:1, one launch (start us, length us, event | category | flops | bytes accessed | tf_op | source)
XLA Modules:
  0.0 43.1 jit_solution(1430345370894034985)
XLA Ops:
  0.6 6.9 %collective-permute-start.1 = (f32[1,3,1024]{2,0,1:T(1,128)}, f32[1,3,1024]{2,0,1:T(1,128)S(1)}, u32[]{:S(2)}, u32[]{:S(2)}) collective-permute-start(f32[1,3,1024]{2,0,1:T(1,128)} %param.4), channel_id=1, source_target_pairs={{0,31},{1,0},{2,1},{3,2},{4,3},{5,4},{6,5},{7,6},{8,7},{9,8},{10,9... | collective-permute-start | bytes 36872 | tf_op jit(solution)/shard_map/ppermute | solution.py:295
  7.5 0.0 collective-permute-start
  8.2 0.0 copy-start.1
  8.8 0.0 copy-start
  8.9 0.1 pad.1.clone
  8.9 0.1 pad.2.clone
  9.0 0.0 copy-done.1
  9.0 0.1 add_add_fusion.table_in.whole_ref
  9.1 0.0 collective-permute-done.1
  9.1 2.9 %collective-permute-done = f32[1,3,1024]{2,0,1:T(1,128)S(1)} collective-permute-done((f32[1,3,1024]{2,0,1:T(1,128)}, f32[1,3,1024]{2,0,1:T(1,128)S(1)}, u32[]{:S(2)}, u32[]{:S(2)}) %collective-permute-start) | collective-permute-done | bytes 12320 | tf_op jit(solution)/shard_map/ppermute | solution.py:295
  12.0 0.0 copy-done
  12.0 30.4 %shard_map.59 = (f32[3,3,8,128]{3,2,1,0:T(8,128)S(1)}, f32[1,128]{1,0:T(1,128)S(1)}) custom-call(f32[3,8,128]{2,1,0:T(8,128)S(1)} %bitcast.9, f32[3,8,128]{2,1,0:T(8,128)S(1)} %bitcast.11, f32[3,8,128]{2,1,0:T(8,128)S(1)} %bitcast.10, s32[5,256]{1,0:T(8,128)S(1)} %add_add_fusion.table_in.whole_ref), custom_call_target="tpu_custom_call" | custom-call | tf_op jit(solution)/shard_map/pallas_call | solution.py:299
  42.4 0.7 %shard_map.60 = (f32[3,8,128]{2,1,0:T(8,128)}, f32[1,128]{1,0:T(1,128)}) custom-call(f32[3,3,8,128]{3,2,1,0:T(8,128)S(1)} %get-tuple-element.6.images_ref, f32[1,128]{1,0:T(1,128)S(1)} %get-tuple-element.7.total_ref, s32[5,256]{1,0:T(8,128)S(1)} %add_add_fusion.table_in.whole_ref), custom_call_target="tpu_custom_call" | custom-call | tf_op jit(solution)/shard_map/pallas_call | solution.py:328
Async XLA Ops:
  0.6 8.5 %collective-permute-start.1 = (f32[1,3,1024]{2,0,1:T(1,128)}, f32[1,3,1024]{2,0,1:T(1,128)S(1)}, u32[]{:S(2)}, u32[]{:S(2)}) collective-permute-start(f32[1,3,1024]{2,0,1:T(1,128)} %param.4), channel_id=1, source_target_pairs={{0,31},{1,0},{2,1},{3,2},{4,3},{5,4},{6,5},{7,6},{8,7},{9,8},{10,9... | collective-permute-start | bytes 36872 | tf_op jit(solution)/shard_map/ppermute | solution.py:295
  7.5 4.4 %collective-permute-start = (f32[1,3,1024]{2,0,1:T(1,128)}, f32[1,3,1024]{2,0,1:T(1,128)S(1)}, u32[]{:S(2)}, u32[]{:S(2)}) collective-permute-start(f32[1,3,1024]{2,0,1:T(1,128)} %param.4), channel_id=1, source_target_pairs={{0,1},{1,2},{2,3},{3,4},{4,5},{5,6},{6,7},{7,8},{8,9},{9,10},{10,1... | collective-permute-start | bytes 36872 | tf_op jit(solution)/shard_map/ppermute | solution.py:295
  8.2 0.8 %copy-start.1 = (s32[256,3]{0,1:T(4,128)S(1)}, s32[256,3]{0,1:T(4,128)}, u32[]{:S(2)}) copy-start(s32[256,3]{0,1:T(4,128)} %param.5) | copy-start | bytes 9220
  8.8 3.1 %copy-start = (f32[1,3,1024]{2,0,1:T(1,128)S(1)}, f32[1,3,1024]{2,0,1:T(1,128)}, u32[]{:S(2)}) copy-start(f32[1,3,1024]{2,0,1:T(1,128)} %param.4) | copy-start | bytes 36868

commit v6 on v5

--- a/solution.py
+++ b/solution.py
@@ -52,14 +52,14 @@
     centre = jnp.where(row == 3, -1.0, jnp.where(row == 4, -square, y + y))
     ph, pm, plow = split3(partner)
     ch, cm, cl = split3(centre)
-    a = jnp.concatenate([ph, ph, ph, pm, pm, plow], axis=1)
+    a = jnp.concatenate([ph, ph, ph, pm, pm, plow], axis=1).astype(BF16)
     b = jnp.concatenate([ch, cm, cl, ch, cm, ch], axis=1).astype(BF16)
     x = jnp.concatenate([ph, pm, plow, jnp.zeros_like(y)], axis=1).astype(BF16)
     return a, b, x
 
 
 def kernel(
-    x_ref, left_ref, right_ref, table_in, images_ref, total_ref,
+    x_ref, beside_ref, apart_ref, table_in, images_ref, total_ref,
     table, local_sem, relay_sems, cur, anchor, aop, bop, xop, raw, ahead, halves, far, whole, around, plane, mine, part, parts, sems,
 ):
     image, slab = lax.axis_index("image"), lax.axis_index("space")
@@ -106,7 +106,7 @@
         bop[version, lo : lo + n] = b
         xop[version, lo : lo + n] = x
         for i in range(n):
-            aop[version, lo + i] = a[i].T.astype(BF16)
+            aop[version, lo + i] = a[i].T
 
     def rows(slab_ref, first, last):
         n = last - first
@@ -153,7 +153,10 @@
         for c in range(3):
             ref[c] = y[:, c]
 
-    own, left, right = (rows(ref, 0, NB) * SCALE for ref in (x_ref, left_ref, right_ref))
+    own, apart, partner = (rows(ref, 0, NB) * SCALE for ref in (x_ref, apart_ref, beside_ref))
+    second = lax.rem(slab, 2) == 1
+    left = jnp.where(second, partner, apart)
+    right = jnp.where(second, apart, partner)
     for i, y in enumerate((left, own, right)):
         anchor[1 + i] = y[0]
         store(0, OWN + (i - 1) * NB, y)
@@ -291,9 +294,8 @@
 
 def body(positions, neighbours, brackets, codes):
     vmem = pl.BlockSpec(memory_space=pltpu.VMEM)
-    left, right = (
-        lax.ppermute(positions, "space", [(i, (i + d) % N_SPACE) for i in range(N_SPACE)]) for d in (1, -1)
-    )
+    partner = lax.ppermute(positions, "space", [(i, i + 1 - 2 * (i % 2)) for i in range(N_SPACE)])
+    apart = lax.ppermute(positions, "space", [(i, (i + 2 * (i % 2) - 1) % N_SPACE) for i in range(N_SPACE)])
     along = [jnp.broadcast_to(v[:, None], (1, BLOCKS)) for v in (brackets, codes)]
     whole = jnp.concatenate([neighbours.T] + along, axis=0)
     images, total = pl.pallas_call(
@@ -323,7 +325,7 @@
             pltpu.SemaphoreType.DMA((2, 11)),
         ],
         compiler_params=pltpu.CompilerParams(collective_id=0, has_side_effects=True, vmem_limit_bytes=48 << 20),
-    )(*(x.reshape(3, NB, BLOCK) for x in (positions, left, right)), whole)
+    )(*(x.reshape(3, NB, BLOCK) for x in (positions, partner, apart)), whole)
     hbm = pl.BlockSpec(memory_space=pl.ANY)
     out, fraction = pl.pallas_call(
         blend,

time: 43.3 us -> 47.1 us (1.088)
  starting transfers between devices: 6.89 us -> 14.3 us
  waiting for transfers between devices: 2.88 us -> 0.01 us
  Pallas kernels: 31.1 us -> 29.9 us
    ppermute x2, starting transfers between devices: 6.89 us -> 14.3 us  [the longest x1 9.32 us: body(): lax.ppermute(positions, 'space', [(i, i + 1 - 2 * (i % 2)) for i in range...]
    ppermute x2, waiting for transfers between devices: 2.88 us -> 0.01 us  [the longest x1 0.01 us: body(): lax.ppermute(positions, 'space', [(i, (i + 2 * (i % 2) - 1) % N_SPACE) fo...]
    pallas_call x1, Pallas kernels: 30.4 us -> 29.2 us  [body(): pl.pallas_call(kernel, out_shape=(jax.ShapeDtypeStruct((3, 3, NB, BLOCK),...]
  transfers between devices with their start and end apart: 2 -> 2, of which waited for: 1 -> 0; matrix products, arithmetic and copies ran while one was open for 1% -> 0% of each run, Pallas kernels for 0% -> 0%
where the time goes in v6:
time: 47.1 us; the launch traced here: 46.8 us
  Pallas kernels  29.9 us (63%)
  starting transfers between devices  14.3 us (30%)
  between operations  1.98 us (4%)
  local copies, waits for them, and re-layouts  0.62 us (1%)
    pallas_call x1, Pallas kernels, body(): pl.pallas_call(kernel, out_shape=(jax.ShapeDtypeStruct((3, 3, NB, BLOCK),...  29.2 us
    ppermute x1, starting transfers between devices, body(): lax.ppermute(positions, 'space', [(i, i + 1 - 2 * (i % 2)) for i in range...  9.32 us
    ppermute x1, starting transfers between devices, body(): lax.ppermute(positions, 'space', [(i, (i + 2 * (i % 2) - 1) % N_SPACE) fo...  4.94 us
  transfers between devices with their start and end apart: 2, of which 0 were waited for; matrix products, arithmetic and copies ran while one was open for 0% of the time, Pallas kernels for 0%

profile of v6, /device:TPU:1, one launch (start us, length us, event | category | flops | bytes accessed | tf_op | source)
XLA Modules:
  0.0 46.8 jit_solution(11552421177931763605)
XLA Ops:
  0.6 4.9 %collective-permute-start.1 = (f32[1,3,1024]{2,0,1:T(1,128)}, f32[1,3,1024]{2,0,1:T(1,128)S(1)}, u32[]{:S(2)}, u32[]{:S(2)}) collective-permute-start(f32[1,3,1024]{2,0,1:T(1,128)} %param.4), channel_id=1, source_target_pairs={{0,31},{1,2},{2,1},{3,4},{4,3},{5,6},{6,5},{7,8},{8,7},{9,10},{10,... | collective-permute-start | bytes 36872 | tf_op jit(solution)/shard_map/ppermute | solution.py:298
  5.6 9.3 %collective-permute-start = (f32[1,3,1024]{2,0,1:T(1,128)}, f32[1,3,1024]{2,0,1:T(1,128)S(1)}, u32[]{:S(2)}, u32[]{:S(2)}) collective-permute-start(f32[1,3,1024]{2,0,1:T(1,128)} %param.4), channel_id=1, source_target_pairs={{0,1},{1,0},{2,3},{3,2},{4,5},{5,4},{6,7},{7,6},{8,9},{9,8},{10,11... | collective-permute-start | bytes 36872 | tf_op jit(solution)/shard_map/ppermute | solution.py:297
  15.5 0.0 copy-start.1
  16.2 0.0 copy-start
  16.2 0.1 pad.1.clone
  16.3 0.1 pad.2.clone
  16.4 0.0 copy-done.1
  16.4 0.1 add_add_fusion.table_in.whole_ref
  16.4 0.0 collective-permute-done.1
  16.5 0.0 collective-permute-done
  16.5 0.5 copy-done
  16.9 29.2 %shard_map.59 = (f32[3,3,8,128]{3,2,1,0:T(8,128)S(1)}, f32[1,128]{1,0:T(1,128)S(1)}) custom-call(f32[3,8,128]{2,1,0:T(8,128)S(1)} %bitcast.9, f32[3,8,128]{2,1,0:T(8,128)S(1)} %bitcast.11, f32[3,8,128]{2,1,0:T(8,128)S(1)} %bitcast.10, s32[5,256]{1,0:T(8,128)S(1)} %add_add_fusion.table_in.whole_ref), custom_call_target="tpu_custom_call" | custom-call | tf_op jit(solution)/shard_map/pallas_call | solution.py:301
  46.1 0.7 %shard_map.60 = (f32[3,8,128]{2,1,0:T(8,128)}, f32[1,128]{1,0:T(1,128)}) custom-call(f32[3,3,8,128]{3,2,1,0:T(8,128)S(1)} %get-tuple-element.6.images_ref, f32[1,128]{1,0:T(1,128)S(1)} %get-tuple-element.7.total_ref, s32[5,256]{1,0:T(8,128)S(1)} %add_add_fusion.table_in.whole_ref), custom_call_target="tpu_custom_call" | custom-call | tf_op jit(solution)/shard_map/pallas_call | solution.py:330
Async XLA Ops:
  0.6 15.8 %collective-permute-start.1 = (f32[1,3,1024]{2,0,1:T(1,128)}, f32[1,3,1024]{2,0,1:T(1,128)S(1)}, u32[]{:S(2)}, u32[]{:S(2)}) collective-permute-start(f32[1,3,1024]{2,0,1:T(1,128)} %param.4), channel_id=1, source_target_pairs={{0,31},{1,2},{2,1},{3,4},{4,3},{5,6},{6,5},{7,8},{8,7},{9,10},{10,... | collective-permute-start | bytes 36872 | tf_op jit(solution)/shard_map/ppermute | solution.py:298
  5.6 10.9 %collective-permute-start = (f32[1,3,1024]{2,0,1:T(1,128)}, f32[1,3,1024]{2,0,1:T(1,128)S(1)}, u32[]{:S(2)}, u32[]{:S(2)}) collective-permute-start(f32[1,3,1024]{2,0,1:T(1,128)} %param.4), channel_id=1, source_target_pairs={{0,1},{1,0},{2,3},{3,2},{4,5},{5,4},{6,7},{7,6},{8,9},{9,8},{10,11... | collective-permute-start | bytes 36872 | tf_op jit(solution)/shard_map/ppermute | solution.py:297
  15.5 0.8 %copy-start.1 = (s32[256,3]{0,1:T(4,128)S(1)}, s32[256,3]{0,1:T(4,128)}, u32[]{:S(2)}) copy-start(s32[256,3]{0,1:T(4,128)} %param.5) | copy-start | bytes 9220
  16.2 0.7 %copy-start = (f32[1,3,1024]{2,0,1:T(1,128)S(1)}, f32[1,3,1024]{2,0,1:T(1,128)}, u32[]{:S(2)}) copy-start(f32[1,3,1024]{2,0,1:T(1,128)} %param.4) | copy-start | bytes 36868

commit v7 on v5

--- a/solution.py
+++ b/solution.py
@@ -52,7 +52,7 @@
     centre = jnp.where(row == 3, -1.0, jnp.where(row == 4, -square, y + y))
     ph, pm, plow = split3(partner)
     ch, cm, cl = split3(centre)
-    a = jnp.concatenate([ph, ph, ph, pm, pm, plow], axis=1)
+    a = jnp.concatenate([ph, ph, ph, pm, pm, plow], axis=1).astype(BF16)
     b = jnp.concatenate([ch, cm, cl, ch, cm, ch], axis=1).astype(BF16)
     x = jnp.concatenate([ph, pm, plow, jnp.zeros_like(y)], axis=1).astype(BF16)
     return a, b, x
@@ -106,7 +106,7 @@
         bop[version, lo : lo + n] = b
         xop[version, lo : lo + n] = x
         for i in range(n):
-            aop[version, lo + i] = a[i].T.astype(BF16)
+            aop[version, lo + i] = a[i].T
 
     def rows(slab_ref, first, last):
         n = last - first
@@ -182,25 +182,56 @@
     last = send(halves.at[0], right2, 4, beside(-2))
     last.start()
     store(0, OWN, y)
-    inner = (OWN + HALO, NB - 2 * HALO)
-    store(1, inner[0], step(0, inner))
+
+    def advance(version, *runs):
+        y = step(version, *runs)
+        at = 0
+        for lo, n in runs:
+            store(version + 1, lo, y[at : at + n])
+            at += n
+
+    def take_left2():
+        middle[0].wait_recv()
+        return rows(left2, 0, NB // 2)
+
+    def take_left():
+        middle[1].wait_recv()
+        return jnp.concatenate([rows(left.at[h], 0, NB // 2) for h in range(2)], axis=0)
+
+    def take_right():
+        middle[2].wait_recv()
+        store(0, OWN + NB, jnp.concatenate([rows(right.at[0], 0, NB // 2), rows(right.at[1], 0, 1)], axis=0))
+
+    second = lax.rem(slab, 2) == 1
+
+    @pl.when(jnp.logical_not(second))
+    def _():
+        take_right()
+        advance(0, (OWN + 2, 9))
+        advance(1, (OWN + 4, 5))
+        advance(2, (OWN + 6, 1))
+        store(0, OWN - NB - NB // 2, jnp.concatenate([take_left2(), take_left()], axis=0))
+        for s in range(3):
+            advance(s, (OWN - 10 + 2 * s, 12))
+
+    @pl.when(second)
+    def _():
+        store(0, OWN - NB, take_left())
+        advance(0, (OWN - 6, 12))
+        advance(1, (OWN - 4, 8))
+        advance(2, (OWN - 2, 4))
+        store(0, OWN - NB - NB // 2, take_left2())
+        take_right()
+        for s in range(3):
+            advance(s, (OWN - 10 + 2 * s, 4), (OWN + 6 - 2 * s, 5))
+
     for c in middle:
-        c.wait()
+        c.wait_send()
     relay(1)
-    left = jnp.concatenate([rows(left2, 0, NB // 2)] + [rows(left.at[h], 0, NB // 2) for h in range(2)], axis=0)
-    store(0, OWN - NB - NB // 2, left)
-    store(0, OWN + NB, jnp.concatenate([rows(right.at[0], 0, NB // 2), rows(right.at[1], 0, 1)], axis=0))
-
-    for s in range(1, LAST + 1):
+
+    for s in range(4, LAST + 1):
         reach = HALO * (LAST - s)
         lo, end = OWN - reach, OWN + reach + 1
-        if s == 1:
-            n = inner[0] - lo
-            after = inner[0] + inner[1]
-            head = step(0, (lo, n), (after, end - after))
-            store(1, lo, head[:n])
-            store(1, after, head[n:])
-            continue
         head = step(s - 1, (lo, end - lo))
         if s < LAST:
             store(s, lo, head)

time: 43.3 us -> 44.1 us (1.018)
  Pallas kernels: 31.1 us -> 31.7 us
    pallas_call x1, Pallas kernels: 30.4 us -> 31 us  [body(): pl.pallas_call(kernel, out_shape=(jax.ShapeDtypeStruct((3, 3, NB, BLOCK),...]
  transfers between devices with their start and end apart: 2 -> 2, of which waited for: 1 -> 1; matrix products, arithmetic and copies ran while one was open for 1% -> 0% of each run, Pallas kernels for 0% -> 0%
where the time goes in v7:
time: 44.1 us; the launch traced here: 43.9 us
  Pallas kernels  31.7 us (72%)
  starting transfers between devices  6.89 us (16%)
  waiting for transfers between devices  2.88 us (7%)
  between operations  2.13 us (5%)
    pallas_call x1, Pallas kernels, body(): pl.pallas_call(kernel, out_shape=(jax.ShapeDtypeStruct((3, 3, NB, BLOCK),...  31 us
    ppermute x2, starting transfers between devices, body(): lax.ppermute(positions, 'space', [(i, (i + d) % N_SPACE) for i in range(N...  6.89 us
    ppermute x2, waiting for transfers between devices, body(): lax.ppermute(positions, 'space', [(i, (i + d) % N_SPACE) for i in range(N...  2.88 us
  transfers between devices with their start and end apart: 2, of which 1 were waited for; matrix products, arithmetic and copies ran while one was open for 0% of the time, Pallas kernels for 0%

profile of v7, /device:TPU:1, one launch (start us, length us, event | category | flops | bytes accessed | tf_op | source)
XLA Modules:
  0.0 43.9 jit_solution(14223972966542766402)
XLA Ops:
  0.6 6.9 %collective-permute-start.1 = (f32[1,3,1024]{2,0,1:T(1,128)}, f32[1,3,1024]{2,0,1:T(1,128)S(1)}, u32[]{:S(2)}, u32[]{:S(2)}) collective-permute-start(f32[1,3,1024]{2,0,1:T(1,128)} %param.4), channel_id=1, source_target_pairs={{0,31},{1,0},{2,1},{3,2},{4,3},{5,4},{6,5},{7,6},{8,7},{9,8},{10,9... | collective-permute-start | bytes 36872 | tf_op jit(solution)/shard_map/ppermute | solution.py:326
  7.5 0.0 collective-permute-start
  8.2 0.0 copy-start.1
  8.8 0.0 copy-start
  8.9 0.1 pad.1.clone
  8.9 0.1 pad.2.clone
  9.0 0.0 copy-done.1
  9.0 0.1 add_add_fusion.table_in.whole_ref
  9.1 0.0 collective-permute-done.1
  9.1 2.9 %collective-permute-done = f32[1,3,1024]{2,0,1:T(1,128)S(1)} collective-permute-done((f32[1,3,1024]{2,0,1:T(1,128)}, f32[1,3,1024]{2,0,1:T(1,128)S(1)}, u32[]{:S(2)}, u32[]{:S(2)}) %collective-permute-start) | collective-permute-done | bytes 12320 | tf_op jit(solution)/shard_map/ppermute | solution.py:326
  12.0 0.0 copy-done
  12.0 31.0 %shard_map.59 = (f32[3,3,8,128]{3,2,1,0:T(8,128)S(1)}, f32[1,128]{1,0:T(1,128)S(1)}) custom-call(f32[3,8,128]{2,1,0:T(8,128)S(1)} %bitcast.9, f32[3,8,128]{2,1,0:T(8,128)S(1)} %bitcast.11, f32[3,8,128]{2,1,0:T(8,128)S(1)} %bitcast.10, s32[5,256]{1,0:T(8,128)S(1)} %add_add_fusion.table_in.whole_ref), custom_call_target="tpu_custom_call" | custom-call | tf_op jit(solution)/shard_map/pallas_call | solution.py:330
  43.0 0.7 %shard_map.60 = (f32[3,8,128]{2,1,0:T(8,128)}, f32[1,128]{1,0:T(1,128)}) custom-call(f32[3,3,8,128]{3,2,1,0:T(8,128)S(1)} %get-tuple-element.6.images_ref, f32[1,128]{1,0:T(1,128)S(1)} %get-tuple-element.7.total_ref, s32[5,256]{1,0:T(8,128)S(1)} %add_add_fusion.table_in.whole_ref), custom_call_target="tpu_custom_call" | custom-call | tf_op jit(solution)/shard_map/pallas_call | solution.py:359
Async XLA Ops:
  0.6 8.5 %collective-permute-start.1 = (f32[1,3,1024]{2,0,1:T(1,128)}, f32[1,3,1024]{2,0,1:T(1,128)S(1)}, u32[]{:S(2)}, u32[]{:S(2)}) collective-permute-start(f32[1,3,1024]{2,0,1:T(1,128)} %param.4), channel_id=1, source_target_pairs={{0,31},{1,0},{2,1},{3,2},{4,3},{5,4},{6,5},{7,6},{8,7},{9,8},{10,9... | collective-permute-start | bytes 36872 | tf_op jit(solution)/shard_map/ppermute | solution.py:326
  7.5 4.4 %collective-permute-start = (f32[1,3,1024]{2,0,1:T(1,128)}, f32[1,3,1024]{2,0,1:T(1,128)S(1)}, u32[]{:S(2)}, u32[]{:S(2)}) collective-permute-start(f32[1,3,1024]{2,0,1:T(1,128)} %param.4), channel_id=1, source_target_pairs={{0,1},{1,2},{2,3},{3,4},{4,5},{5,6},{6,7},{7,8},{8,9},{9,10},{10,1... | collective-permute-start | bytes 36872 | tf_op jit(solution)/shard_map/ppermute | solution.py:326
  8.2 0.8 %copy-start.1 = (s32[256,3]{0,1:T(4,128)S(1)}, s32[256,3]{0,1:T(4,128)}, u32[]{:S(2)}) copy-start(s32[256,3]{0,1:T(4,128)} %param.5) | copy-start | bytes 9220
  8.8 3.1 %copy-start = (f32[1,3,1024]{2,0,1:T(1,128)S(1)}, f32[1,3,1024]{2,0,1:T(1,128)}, u32[]{:S(2)}) copy-start(f32[1,3,1024]{2,0,1:T(1,128)} %param.4) | copy-start | bytes 36868

commit v8 on v5

--- a/solution.py
+++ b/solution.py
@@ -52,7 +52,7 @@
     centre = jnp.where(row == 3, -1.0, jnp.where(row == 4, -square, y + y))
     ph, pm, plow = split3(partner)
     ch, cm, cl = split3(centre)
-    a = jnp.concatenate([ph, ph, ph, pm, pm, plow], axis=1)
+    a = jnp.concatenate([ph, ph, ph, pm, pm, plow], axis=1).astype(BF16)
     b = jnp.concatenate([ch, cm, cl, ch, cm, ch], axis=1).astype(BF16)
     x = jnp.concatenate([ph, pm, plow, jnp.zeros_like(y)], axis=1).astype(BF16)
     return a, b, x
@@ -106,7 +106,7 @@
         bop[version, lo : lo + n] = b
         xop[version, lo : lo + n] = x
         for i in range(n):
-            aop[version, lo + i] = a[i].T.astype(BF16)
+            aop[version, lo + i] = a[i].T
 
     def rows(slab_ref, first, last):
         n = last - first

time: 43.3 us -> 42.9 us (level)
  no operation moved by 1% of the time
where the time goes in v8:
time: 42.9 us; the launch traced here: 42.7 us
  Pallas kernels  30.8 us (72%)
  starting transfers between devices  6.89 us (16%)
  waiting for transfers between devices  2.88 us (7%)
  between operations  1.97 us (5%)
    pallas_call x1, Pallas kernels, body(): pl.pallas_call(kernel, out_shape=(jax.ShapeDtypeStruct((3, 3, NB, BLOCK),...  30 us
    ppermute x2, starting transfers between devices, body(): lax.ppermute(positions, 'space', [(i, (i + d) % N_SPACE) for i in range(N...  6.89 us
    ppermute x2, waiting for transfers between devices, body(): lax.ppermute(positions, 'space', [(i, (i + d) % N_SPACE) for i in range(N...  2.88 us
  transfers between devices with their start and end apart: 2, of which 1 were waited for; matrix products, arithmetic and copies ran while one was open for 1% of the time, Pallas kernels for 0%

profile of v8, /device:TPU:1, one launch (start us, length us, event | category | flops | bytes accessed | tf_op | source)
XLA Modules:
  0.0 42.7 jit_solution(5559808021192668189)
XLA Ops:
  0.6 6.9 %collective-permute-start.1 = (f32[1,3,1024]{2,0,1:T(1,128)}, f32[1,3,1024]{2,0,1:T(1,128)S(1)}, u32[]{:S(2)}, u32[]{:S(2)}) collective-permute-start(f32[1,3,1024]{2,0,1:T(1,128)} %param.4), channel_id=1, source_target_pairs={{0,31},{1,0},{2,1},{3,2},{4,3},{5,4},{6,5},{7,6},{8,7},{9,8},{10,9... | collective-permute-start | bytes 36872 | tf_op jit(solution)/shard_map/ppermute | solution.py:295
  7.5 0.0 collective-permute-start
  8.2 0.0 copy-start.1
  8.8 0.0 copy-start
  8.9 0.1 pad.1.clone
  8.9 0.1 pad.2.clone
  9.0 0.0 copy-done.1
  9.0 0.1 add_add_fusion.table_in.whole_ref
  9.1 0.0 collective-permute-done.1
  9.1 2.9 %collective-permute-done = f32[1,3,1024]{2,0,1:T(1,128)S(1)} collective-permute-done((f32[1,3,1024]{2,0,1:T(1,128)}, f32[1,3,1024]{2,0,1:T(1,128)S(1)}, u32[]{:S(2)}, u32[]{:S(2)}) %collective-permute-start) | collective-permute-done | bytes 12320 | tf_op jit(solution)/shard_map/ppermute | solution.py:295
  12.0 0.0 copy-done
  12.0 30.0 %shard_map.59 = (f32[3,3,8,128]{3,2,1,0:T(8,128)S(1)}, f32[1,128]{1,0:T(1,128)S(1)}) custom-call(f32[3,8,128]{2,1,0:T(8,128)S(1)} %bitcast.9, f32[3,8,128]{2,1,0:T(8,128)S(1)} %bitcast.11, f32[3,8,128]{2,1,0:T(8,128)S(1)} %bitcast.10, s32[5,256]{1,0:T(8,128)S(1)} %add_add_fusion.table_in.whole_ref), custom_call_target="tpu_custom_call" | custom-call | tf_op jit(solution)/shard_map/pallas_call | solution.py:299
  42.0 0.7 %shard_map.60 = (f32[3,8,128]{2,1,0:T(8,128)}, f32[1,128]{1,0:T(1,128)}) custom-call(f32[3,3,8,128]{3,2,1,0:T(8,128)S(1)} %get-tuple-element.6.images_ref, f32[1,128]{1,0:T(1,128)S(1)} %get-tuple-element.7.total_ref, s32[5,256]{1,0:T(8,128)S(1)} %add_add_fusion.table_in.whole_ref), custom_call_target="tpu_custom_call" | custom-call | tf_op jit(solution)/shard_map/pallas_call | solution.py:328
Async XLA Ops:
  0.6 8.5 %collective-permute-start.1 = (f32[1,3,1024]{2,0,1:T(1,128)}, f32[1,3,1024]{2,0,1:T(1,128)S(1)}, u32[]{:S(2)}, u32[]{:S(2)}) collective-permute-start(f32[1,3,1024]{2,0,1:T(1,128)} %param.4), channel_id=1, source_target_pairs={{0,31},{1,0},{2,1},{3,2},{4,3},{5,4},{6,5},{7,6},{8,7},{9,8},{10,9... | collective-permute-start | bytes 36872 | tf_op jit(solution)/shard_map/ppermute | solution.py:295
  7.5 4.4 %collective-permute-start = (f32[1,3,1024]{2,0,1:T(1,128)}, f32[1,3,1024]{2,0,1:T(1,128)S(1)}, u32[]{:S(2)}, u32[]{:S(2)}) collective-permute-start(f32[1,3,1024]{2,0,1:T(1,128)} %param.4), channel_id=1, source_target_pairs={{0,1},{1,2},{2,3},{3,4},{4,5},{5,6},{6,7},{7,8},{8,9},{9,10},{10,1... | collective-permute-start | bytes 36872 | tf_op jit(solution)/shard_map/ppermute | solution.py:295
  8.2 0.8 %copy-start.1 = (s32[256,3]{0,1:T(4,128)S(1)}, s32[256,3]{0,1:T(4,128)}, u32[]{:S(2)}) copy-start(s32[256,3]{0,1:T(4,128)} %param.5) | copy-start | bytes 9220
  8.8 3.1 %copy-start = (f32[1,3,1024]{2,0,1:T(1,128)S(1)}, f32[1,3,1024]{2,0,1:T(1,128)}, u32[]{:S(2)}) copy-start(f32[1,3,1024]{2,0,1:T(1,128)} %param.4) | copy-start | bytes 36868

commit v9 on v8

--- a/solution.py
+++ b/solution.py
@@ -59,7 +59,7 @@
 
 
 def kernel(
-    x_ref, left_ref, right_ref, table_in, images_ref, total_ref,
+    x_ref, right_ref, left_ref, table_in, images_ref, total_ref,
     table, local_sem, relay_sems, cur, anchor, aop, bop, xop, raw, ahead, halves, far, whole, around, plane, mine, part, parts, sems,
 ):
     image, slab = lax.axis_index("image"), lax.axis_index("space")
@@ -323,7 +323,7 @@
             pltpu.SemaphoreType.DMA((2, 11)),
         ],
         compiler_params=pltpu.CompilerParams(collective_id=0, has_side_effects=True, vmem_limit_bytes=48 << 20),
-    )(*(x.reshape(3, NB, BLOCK) for x in (positions, left, right)), whole)
+    )(*(x.reshape(3, NB, BLOCK) for x in (positions, right, left)), whole)
     hbm = pl.BlockSpec(memory_space=pl.ANY)
     out, fraction = pl.pallas_call(
         blend,

time: 42.9 us -> 45.2 us (1.054)
  Pallas kernels: 30.8 us -> 35.4 us
  waiting for transfers between devices: 2.88 us -> 0.01 us
  local copies, waits for them, and re-layouts: 0.16 us -> 0.62 us
    pallas_call x1, Pallas kernels: 30 us -> 34.7 us  [body(): pl.pallas_call(kernel, out_shape=(jax.ShapeDtypeStruct((3, 3, NB, BLOCK),...]
    ppermute x2, waiting for transfers between devices: 2.88 us -> 0.01 us  [body(): lax.ppermute(positions, 'space', [(i, (i + d) % N_SPACE) for i in range(N...]
    unnamed x4, local copies, waits for them, and re-layouts: 0.01 us -> 0.47 us
  transfers between devices with their start and end apart: 2 -> 2, of which waited for: 1 -> 0; matrix products, arithmetic and copies ran while one was open for 1% -> 0% of each run, Pallas kernels for 0% -> 0%
where the time goes in v9:
time: 45.2 us; the launch traced here: 45 us
  Pallas kernels  35.4 us (78%)
  starting transfers between devices  6.92 us (15%)
  between operations  1.97 us (4%)
  local copies, waits for them, and re-layouts  0.62 us (1%)
    pallas_call x1, Pallas kernels, body(): pl.pallas_call(kernel, out_shape=(jax.ShapeDtypeStruct((3, 3, NB, BLOCK),...  34.7 us
    ppermute x2, starting transfers between devices, body(): lax.ppermute(positions, 'space', [(i, (i + d) % N_SPACE) for i in range(N...  6.92 us
  transfers between devices with their start and end apart: 2, of which 0 were waited for; matrix products, arithmetic and copies ran while one was open for 0% of the time, Pallas kernels for 0%

profile of v9, /device:TPU:1, one launch (start us, length us, event | category | flops | bytes accessed | tf_op | source)
XLA Modules:
  0.0 45.0 jit_solution(10353405323547076408)
XLA Ops:
  0.6 3.0 %collective-permute-start.1 = (f32[1,3,1024]{2,0,1:T(1,128)}, f32[1,3,1024]{2,0,1:T(1,128)S(1)}, u32[]{:S(2)}, u32[]{:S(2)}) collective-permute-start(f32[1,3,1024]{2,0,1:T(1,128)} %param.4), channel_id=1, source_target_pairs={{0,1},{1,2},{2,3},{3,4},{4,5},{5,6},{6,7},{7,8},{8,9},{9,10},{10,1... | collective-permute-start | bytes 36872 | tf_op jit(solution)/shard_map/ppermute | solution.py:295
  3.7 3.9 %collective-permute-start = (f32[1,3,1024]{2,0,1:T(1,128)}, f32[1,3,1024]{2,0,1:T(1,128)S(1)}, u32[]{:S(2)}, u32[]{:S(2)}) collective-permute-start(f32[1,3,1024]{2,0,1:T(1,128)} %param.4), channel_id=1, source_target_pairs={{0,31},{1,0},{2,1},{3,2},{4,3},{5,4},{6,5},{7,6},{8,7},{9,8},{10,9... | collective-permute-start | bytes 36872 | tf_op jit(solution)/shard_map/ppermute | solution.py:295
  8.2 0.0 copy-start.1
  8.9 0.0 copy-start
  8.9 0.1 pad.1.clone
  9.0 0.1 pad.2.clone
  9.0 0.0 copy-done.1
  9.0 0.1 add_add_fusion.table_in.whole_ref
  9.1 0.0 collective-permute-done.1
  9.1 0.0 collective-permute-done
  9.1 0.5 %copy-done = f32[1,3,1024]{2,0,1:T(1,128)S(1)} copy-done((f32[1,3,1024]{2,0,1:T(1,128)S(1)}, f32[1,3,1024]{2,0,1:T(1,128)}, u32[]{:S(2)}) %copy-start) | copy-done | bytes 12312
  9.6 34.7 %shard_map.59 = (f32[3,3,8,128]{3,2,1,0:T(8,128)S(1)}, f32[1,128]{1,0:T(1,128)S(1)}) custom-call(f32[3,8,128]{2,1,0:T(8,128)S(1)} %bitcast.9, f32[3,8,128]{2,1,0:T(8,128)S(1)} %bitcast.11, f32[3,8,128]{2,1,0:T(8,128)S(1)} %bitcast.10, s32[5,256]{1,0:T(8,128)S(1)} %add_add_fusion.table_in.whole_ref), custom_call_target="tpu_custom_call" | custom-call | tf_op jit(solution)/shard_map/pallas_call | solution.py:299
  44.2 0.7 %shard_map.60 = (f32[3,8,128]{2,1,0:T(8,128)}, f32[1,128]{1,0:T(1,128)}) custom-call(f32[3,3,8,128]{3,2,1,0:T(8,128)S(1)} %get-tuple-element.6.images_ref, f32[1,128]{1,0:T(1,128)S(1)} %get-tuple-element.7.total_ref, s32[5,256]{1,0:T(8,128)S(1)} %add_add_fusion.table_in.whole_ref), custom_call_target="tpu_custom_call" | custom-call | tf_op jit(solution)/shard_map/pallas_call | solution.py:328
Async XLA Ops:
  0.6 8.5 %collective-permute-start.1 = (f32[1,3,1024]{2,0,1:T(1,128)}, f32[1,3,1024]{2,0,1:T(1,128)S(1)}, u32[]{:S(2)}, u32[]{:S(2)}) collective-permute-start(f32[1,3,1024]{2,0,1:T(1,128)} %param.4), channel_id=1, source_target_pairs={{0,1},{1,2},{2,3},{3,4},{4,5},{5,6},{6,7},{7,8},{8,9},{9,10},{10,1... | collective-permute-start | bytes 36872 | tf_op jit(solution)/shard_map/ppermute | solution.py:295
  3.7 5.4 %collective-permute-start = (f32[1,3,1024]{2,0,1:T(1,128)}, f32[1,3,1024]{2,0,1:T(1,128)S(1)}, u32[]{:S(2)}, u32[]{:S(2)}) collective-permute-start(f32[1,3,1024]{2,0,1:T(1,128)} %param.4), channel_id=1, source_target_pairs={{0,31},{1,0},{2,1},{3,2},{4,3},{5,4},{6,5},{7,6},{8,7},{9,8},{10,9... | collective-permute-start | bytes 36872 | tf_op jit(solution)/shard_map/ppermute | solution.py:295
  8.2 0.8 %copy-start.1 = (s32[256,3]{0,1:T(4,128)S(1)}, s32[256,3]{0,1:T(4,128)}, u32[]{:S(2)}) copy-start(s32[256,3]{0,1:T(4,128)} %param.5) | copy-start | bytes 9220
  8.9 0.7 %copy-start = (f32[1,3,1024]{2,0,1:T(1,128)S(1)}, f32[1,3,1024]{2,0,1:T(1,128)}, u32[]{:S(2)}) copy-start(f32[1,3,1024]{2,0,1:T(1,128)} %param.4) | copy-start | bytes 36868
